TPU v7x, 32 devices: a whole 2x2x4 slice. The times are simulated.
32 devices in a mesh: row: 8 (over z, y), col: 4 (over x, core).
Axes of the slice: x: 2, y: 2, z: 4, core: 2. Of those that a mesh axis runs over, the one named last changes fastest.
Arguments:
- queries: bfloat16 [1, 8, 8, 64, 2048], P(None, 'row', 'col'), may hold values from -17 to 17
- keys: bfloat16 [1, 8, 8, 64, 2048], P(None, 'row', 'col'), may hold values from -5.5 to 5.5
- values: bfloat16 [1, 8, 8, 64, 2048], P(None, 'row', 'col'), may hold values from -6 to 6
- pool_keys: bfloat16 [64, 16, 2048], P(('row', 'col')), may hold values from -6 to 6
- pool_values: bfloat16 [64, 16, 2048], P(('row', 'col')), may hold values from -6 to 6
- top_keys: bfloat16 [1, 32, 2048], P(None, 'col'), may hold values from -6 to 6
- top_values: bfloat16 [1, 32, 2048], P(None, 'col'), may hold values from -6 to 6
- coarse_ids: int32 [1, 8, 8, 8], P(None, 'row', 'col'), may hold values from 0 to 63, as said below
Outputs:
- attended: bfloat16 [1, 8, 8, 64, 2048], P(None, 'row', 'col')
Inputs may be any that keep to these rules, and one draw needn't show every extreme that they name: Entry coarse_ids[n, i, j, c] names a pool block held by the device that holds fine block (i, j) or by one of its eight neighbours in the mesh (no wrap); the device with row index r and col index q holds pool blocks (r * 4 + q) * 2 to (r * 4 + q + 1) * 2 - 1. The 8 entries of a fine block differ.
All inputs are finite; a program needn't handle non-finite values.
Results may differ from a plain program's by a relative error of at most 0.0049.
Values may be sent and summed in bfloat16 or wider, within the bound.
A program may use at most 64 MiB of HBM per device.

v0:
```python
import math

import jax
import jax.numpy as jnp
from jax import lax
from jax.sharding import PartitionSpec as P

HEADS = 16


NEG_FILL = -1e30


def extended(block, sides, width):
    for axis, dim in sides:
        count = lax.axis_size(axis)
        forward = [(i, i + 1) for i in range(count - 1)]
        backward = [(target, source) for source, target in forward]
        low = lax.ppermute(
            lax.slice_in_dim(block, block.shape[dim] - width, None, axis=dim), axis, forward
        )
        high = lax.ppermute(lax.slice_in_dim(block, 0, width, axis=dim), axis, backward)
        block = jnp.concatenate([low, block, high], axis=dim)
    return block


def body(queries, keys, values, pool_keys, pool_values, top_keys, top_values, coarse_ids):
    images, brow_count, bcol_count, block_tokens, model_width = queries.shape
    head_count = HEADS
    head_width = model_width // head_count
    score_scale = 1.0 / math.sqrt(head_width)
    pool_blocks = pool_keys.shape[0]
    pool_tokens = pool_keys.shape[1]
    row_count = lax.axis_size("row")
    col_count = lax.axis_size("col")
    row_index = lax.axis_index("row")
    col_index = lax.axis_index("col")
    pool_key_grid = pool_keys.reshape(1, 1, 1, pool_blocks * pool_tokens, model_width)
    pool_value_grid = pool_values.reshape(1, 1, 1, pool_blocks * pool_tokens, model_width)
    near_keys, near_values = (
        extended(keys, (("row", 1), ("col", 2)), 1),
        extended(values, (("row", 1), ("col", 2)), 1),
    )
    around_keys, around_values = (
        extended(pool_key_grid, (("row", 1), ("col", 2)), 1),
        extended(pool_value_grid, (("row", 1), ("col", 2)), 1),
    )
    around_keys = around_keys.reshape(9 * pool_blocks, pool_tokens, model_width)
    around_values = around_values.reshape(9 * pool_blocks, pool_tokens, model_width)
    top_all_keys, top_all_values = (
        lax.all_gather(top_keys, "col", axis=1, tiled=True),
        lax.all_gather(top_values, "col", axis=1, tiled=True),
    )
    owner_device = coarse_ids // pool_blocks
    owner_row = owner_device // col_count
    owner_col = owner_device % col_count
    local_slot = (
        (owner_row - row_index + 1) * 3 + (owner_col - col_index + 1)
    ) * pool_blocks + coarse_ids % pool_blocks
    global_row = row_index * brow_count + jnp.arange(brow_count, dtype=jnp.int32)
    global_col = col_index * bcol_count + jnp.arange(bcol_count, dtype=jnp.int32)
    total_rows = brow_count * row_count
    total_cols = bcol_count * col_count
    blocks = brow_count * bcol_count
    coarse_length = coarse_ids.shape[-1] * pool_tokens
    valid_parts = []
    for row_step in range(3):
        row_valid = (global_row + row_step - 1 >= 0) & (global_row + row_step - 1 < total_rows)
        for col_step in range(3):
            col_valid = (global_col + col_step - 1 >= 0) & (global_col + col_step - 1 < total_cols)
            part_valid = (row_valid[:, None] & col_valid[None, :]).reshape(blocks, 1)
            valid_parts.append(jnp.broadcast_to(part_valid, (blocks, block_tokens)))
    valid_parts.append(jnp.ones((blocks, coarse_length), dtype=bool))
    list_valid = jnp.concatenate(valid_parts, axis=1).reshape(blocks, 1, 1, -1)

    def attend_image(image_items):
        query_image, key_image, value_image, slot_image, top_key_image, top_value_image = (
            image_items
        )
        query_heads = query_image.reshape(blocks, block_tokens, head_count, head_width)
        key_lists = []
        value_lists = []
        for row_step in range(3):
            for col_step in range(3):
                key_lists.append(
                    key_image[
                        row_step : row_step + brow_count, col_step : col_step + bcol_count
                    ].reshape(blocks, block_tokens, model_width)
                )
                value_lists.append(
                    value_image[
                        row_step : row_step + brow_count, col_step : col_step + bcol_count
                    ].reshape(blocks, block_tokens, model_width)
                )
        key_lists.append(around_keys[slot_image].reshape(blocks, coarse_length, model_width))
        value_lists.append(around_values[slot_image].reshape(blocks, coarse_length, model_width))
        key_list = jnp.concatenate(key_lists, axis=1).reshape(blocks, -1, head_count, head_width)
        value_list = jnp.concatenate(value_lists, axis=1).reshape(
            blocks, -1, head_count, head_width
        )
        near_scores = (
            jnp.einsum("bqhd,bkhd->bhqk", query_heads, key_list, preferred_element_type=jnp.float32)
            * score_scale
        )
        near_scores = jnp.where(list_valid, near_scores, NEG_FILL)
        top_key_heads = top_key_image.reshape(-1, head_count, head_width)
        top_value_heads = top_value_image.reshape(-1, head_count, head_width)
        top_scores = (
            jnp.einsum(
                "bqhd,khd->bhqk", query_heads, top_key_heads, preferred_element_type=jnp.float32
            )
            * score_scale
        )
        row_peak = jnp.maximum(
            jnp.max(near_scores, axis=-1, keepdims=True),
            jnp.max(top_scores, axis=-1, keepdims=True),
        )
        near_exponent = jnp.exp(near_scores - row_peak)
        top_exponent = jnp.exp(top_scores - row_peak)
        row_total = jnp.sum(near_exponent, axis=-1, keepdims=True) + jnp.sum(
            top_exponent, axis=-1, keepdims=True
        )
        near_weights = (near_exponent / row_total).astype(jnp.bfloat16)
        top_weights = (top_exponent / row_total).astype(jnp.bfloat16)
        result = jnp.einsum(
            "bhqk,bkhd->bqhd", near_weights, value_list, preferred_element_type=jnp.float32
        )
        result = result + jnp.einsum(
            "bhqk,khd->bqhd", top_weights, top_value_heads, preferred_element_type=jnp.float32
        )
        return result.reshape(brow_count, bcol_count, block_tokens, model_width).astype(
            jnp.bfloat16
        )

    return lax.map(
        attend_image, (queries, near_keys, near_values, local_slot, top_all_keys, top_all_values)
    )


def solution(mesh):
    placed = (
        P(None, "row", "col", None, None),
        P(None, "row", "col", None, None),
        P(None, "row", "col", None, None),
        P(("row", "col"), None, None),
        P(("row", "col"), None, None),
        P(None, "col", None),
        P(None, "col", None),
        P(None, "row", "col", None),
    )
    return jax.shard_map(
        body,
        mesh=mesh,
        in_specs=placed,
        out_specs=P(None, "row", "col", None, None),
        check_vma=False,
    )
```

profile of v0, /device:TPU:5, one launch (start us, length us, event | category | flops | bytes accessed | tf_op | source)
XLA Modules:
  0.0 116.4 jit_solution(13526453284562500856)
XLA Ops:
  0.0 3.3 %collective-permute-start = (bf16[1,1,2,64,2048]{4,3,2,1,0:T(8,128)(2,1)}, bf16[1,1,2,64,2048]{4,3,2,1,0:T(8,128)(2,1)S(1)}, u32[]{:S(2)}, u32[]{:S(2)}) collective-permute-start(bf16[1,1,2,64,2048]{4,3,2,1,0:T(8,128)(2,1)} %param.10), channel_id=1, source_target_pairs={{0,4},{4,8},{8,12},{12,16},{16,20},{20,24},{24,28},{1,5},{5,9},{9,... | collective-permute-start | bytes 1572872 | tf_op jit(solution)/shard_map/ppermute | solution.py:19
  3.3 2.2 %collective-permute-start.1 = (bf16[1,1,2,64,2048]{4,3,2,1,0:T(8,128)(2,1)}, bf16[1,1,2,64,2048]{4,3,2,1,0:T(8,128)(2,1)S(1)}, u32[]{:S(2)}, u32[]{:S(2)}) collective-permute-start(bf16[1,1,2,64,2048]{4,3,2,1,0:T(8,128)(2,1)} %param.10), channel_id=1, source_target_pairs={{4,0},{8,4},{12,8},{16,12},{20,16},{24,20},{28,24},{5,1},{9,5},{13... | collective-permute-start | bytes 1572872 | tf_op jit(solution)/shard_map/ppermute | solution.py:22
  5.4 1.9 %collective-permute-start.5 = (bf16[1,1,1,32,2048]{4,3,2,1,0:T(8,128)(2,1)}, bf16[1,1,1,32,2048]{4,3,2,1,0:T(8,128)(2,1)S(1)}, u32[]{:S(2)}, u32[]{:S(2)}) collective-permute-start(bf16[1,1,1,32,2048]{4,3,2,1,0:T(8,128)(2,1)} %bitcast.200), channel_id=1, source_target_pairs={{4,0},{8,4},{12,8},{16,12},{20,16},{24,20},{28,24},{5,1},{9,5},{13... | collective-permute-start | bytes 393224 | tf_op jit(solution)/shard_map/ppermute | solution.py:22
  7.4 4.3 %collective-permute-start.4 = (bf16[1,1,1,32,2048]{4,3,2,1,0:T(8,128)(2,1)}, bf16[1,1,1,32,2048]{4,3,2,1,0:T(8,128)(2,1)S(1)}, u32[]{:S(2)}, u32[]{:S(2)}) collective-permute-start(bf16[1,1,1,32,2048]{4,3,2,1,0:T(8,128)(2,1)} %bitcast.201), channel_id=1, source_target_pairs={{0,4},{4,8},{8,12},{12,16},{16,20},{20,24},{24,28},{1,5},{5,9},{9,... | collective-permute-start | bytes 393224 | tf_op jit(solution)/shard_map/ppermute | solution.py:19
  11.6 1.9 %collective-permute-start.13 = (bf16[1,1,1,32,2048]{4,3,2,1,0:T(8,128)(2,1)}, bf16[1,1,1,32,2048]{4,3,2,1,0:T(8,128)(2,1)S(1)}, u32[]{:S(2)}, u32[]{:S(2)}) collective-permute-start(bf16[1,1,1,32,2048]{4,3,2,1,0:T(8,128)(2,1)} %bitcast.204), channel_id=1, source_target_pairs={{4,0},{8,4},{12,8},{16,12},{20,16},{24,20},{28,24},{5,1},{9,5},{13... | collective-permute-start | bytes 393224 | tf_op jit(solution)/shard_map/ppermute | solution.py:22
  16.2 7.3 %all_gather.6 = bf16[1,32,2048]{2,1,0:T(8,128)(2,1)S(1)} all-gather(bf16[1,8,2048]{2,1,0:T(8,128)(2,1)} %param.13), channel_id=1, replica_groups=mesh['row'=8,'col'=4] {'col'}, dimensions={1}, use_global_device_ids=true | all-gather | bytes 163840 | tf_op jit(solution)/shard_map/all_gather | solution.py:51
  25.0 5.6 %all_gather.7 = bf16[1,32,2048]{2,1,0:T(8,128)(2,1)S(1)} all-gather(bf16[1,8,2048]{2,1,0:T(8,128)(2,1)} %param.14), channel_id=1, replica_groups=mesh['row'=8,'col'=4] {'col'}, dimensions={1}, use_global_device_ids=true | all-gather | bytes 163840 | tf_op jit(solution)/shard_map/all_gather | solution.py:52
  32.6 4.5 %collective-permute-start.12 = (bf16[1,1,1,32,2048]{4,3,2,1,0:T(8,128)(2,1)}, bf16[1,1,1,32,2048]{4,3,2,1,0:T(8,128)(2,1)S(1)}, u32[]{:S(2)}, u32[]{:S(2)}) collective-permute-start(bf16[1,1,1,32,2048]{4,3,2,1,0:T(8,128)(2,1)} %bitcast.205), channel_id=1, source_target_pairs={{0,4},{4,8},{8,12},{12,16},{16,20},{20,24},{24,28},{1,5},{5,9},{9,... | collective-permute-start | bytes 393224 | tf_op jit(solution)/shard_map/ppermute | solution.py:19
  37.2 2.2 %collective-permute-start.8 = (bf16[1,1,2,64,2048]{4,3,2,1,0:T(8,128)(2,1)}, bf16[1,1,2,64,2048]{4,3,2,1,0:T(8,128)(2,1)S(1)}, u32[]{:S(2)}, u32[]{:S(2)}) collective-permute-start(bf16[1,1,2,64,2048]{4,3,2,1,0:T(8,128)(2,1)} %param.9), channel_id=1, source_target_pairs={{0,4},{4,8},{8,12},{12,16},{16,20},{20,24},{24,28},{1,5},{5,9},{9,... | collective-permute-start | bytes 1572872 | tf_op jit(solution)/shard_map/ppermute | solution.py:19
  40.4 3.1 %collective-permute-start.9 = (bf16[1,1,2,64,2048]{4,3,2,1,0:T(8,128)(2,1)}, bf16[1,1,2,64,2048]{4,3,2,1,0:T(8,128)(2,1)S(1)}, u32[]{:S(2)}, u32[]{:S(2)}) collective-permute-start(bf16[1,1,2,64,2048]{4,3,2,1,0:T(8,128)(2,1)} %param.9), channel_id=1, source_target_pairs={{4,0},{8,4},{12,8},{16,12},{20,16},{24,20},{28,24},{5,1},{9,5},{13... | collective-permute-start | bytes 1572872 | tf_op jit(solution)/shard_map/ppermute | solution.py:22
  43.5 3.1 %collective-permute-start.7 = (bf16[1,3,1,32,2048]{4,3,2,1,0:T(8,128)(2,1)S(1)}, bf16[1,3,1,32,2048]{4,3,2,1,0:T(8,128)(2,1)S(1)}, u32[]{:S(2)}, u32[]{:S(2)}) collective-permute-start(bf16[1,3,1,32,2048]{4,3,2,1,0:T(8,128)(2,1)S(1)} %pad_maximum_fusion.3), channel_id=1, source_target_pairs={{1,0},{2,1},{3,2},{5,4},{6,5},{7,6},{9,8},{10,9},{11,10},{13,12},{... | collective-permute-start | bytes 1179656 | tf_op jit(solution)/shard_map/ppermute | solution.py:22
  48.4 3.0 %collective-permute-start.6 = (bf16[1,3,1,32,2048]{4,3,2,1,0:T(8,128)(2,1)S(1)}, bf16[1,3,1,32,2048]{4,3,2,1,0:T(8,128)(2,1)S(1)}, u32[]{:S(2)}, u32[]{:S(2)}) collective-permute-start(bf16[1,3,1,32,2048]{4,3,2,1,0:T(8,128)(2,1)S(1)} %pad_maximum_fusion.3), channel_id=1, source_target_pairs={{0,1},{1,2},{2,3},{4,5},{5,6},{6,7},{8,9},{9,10},{10,11},{12,13},{... | collective-permute-start | bytes 1179656 | tf_op jit(solution)/shard_map/ppermute | solution.py:19
  51.5 1.9 %collective-permute-start.15 = (bf16[1,3,1,32,2048]{4,3,2,1,0:T(8,128)(2,1)}, bf16[1,3,1,32,2048]{4,3,2,1,0:T(8,128)(2,1)}, u32[]{:S(2)}, u32[]{:S(2)}) collective-permute-start(bf16[1,3,1,32,2048]{4,3,2,1,0:T(8,128)(2,1)} %pad_maximum_fusion.2), channel_id=1, source_target_pairs={{1,0},{2,1},{3,2},{5,4},{6,5},{7,6},{9,8},{10,9},{11,10},{13,12},{... | collective-permute-start | bytes 1179656 | tf_op jit(solution)/shard_map/ppermute | solution.py:22
  54.8 8.6 %collective-permute-done.8 = bf16[1,1,2,64,2048]{4,3,2,1,0:T(8,128)(2,1)S(1)} collective-permute-done((bf16[1,1,2,64,2048]{4,3,2,1,0:T(8,128)(2,1)}, bf16[1,1,2,64,2048]{4,3,2,1,0:T(8,128)(2,1)S(1)}, u32[]{:S(2)}, u32[]{:S(2)}) %collective-permute-start.8) | collective-permute-done | bytes 524320 | tf_op jit(solution)/shard_map/ppermute | solution.py:19
  63.3 4.5 %collective-permute-start.14 = (bf16[1,3,1,32,2048]{4,3,2,1,0:T(8,128)(2,1)}, bf16[1,3,1,32,2048]{4,3,2,1,0:T(8,128)(2,1)}, u32[]{:S(2)}, u32[]{:S(2)}) collective-permute-start(bf16[1,3,1,32,2048]{4,3,2,1,0:T(8,128)(2,1)} %pad_maximum_fusion.2), channel_id=1, source_target_pairs={{0,1},{1,2},{2,3},{4,5},{5,6},{6,7},{8,9},{9,10},{10,11},{12,13},{... | collective-permute-start | bytes 1179656 | tf_op jit(solution)/shard_map/ppermute | solution.py:19
  71.0 3.6 %collective-permute-start.2 = (bf16[1,3,1,64,2048]{4,3,2,1,0:T(8,128)(2,1)}, bf16[1,3,1,64,2048]{4,3,2,1,0:T(8,128)(2,1)}, u32[]{:S(2)}, u32[]{:S(2)}) collective-permute-start(bf16[1,3,1,64,2048]{4,3,2,1,0:T(8,128)(2,1)} %get-tuple-element.58), channel_id=1, source_target_pairs={{0,1},{1,2},{2,3},{4,5},{5,6},{6,7},{8,9},{9,10},{10,11},{12,13},{... | collective-permute-start | bytes 2359304 | tf_op jit(solution)/shard_map/ppermute | solution.py:19
  74.7 2.1 %pad_maximum_fusion.1 = bf16[1,3,3,32,2048]{4,3,2,1,0:T(8,128)(2,1)} fusion(bf16[1,3,1,32,2048]{4,3,2,1,0:T(8,128)(2,1)S(1)} %collective-permute-done.7, bf16[1,1,1,32,2048]{4,3,2,1,0:T(8,128)(2,1)} %copy-done.7, bf16[1,1,1,32,2048]{4,3,2,1,0:T(8,128)(2,1)S(1)} %bitcast.203, bf16[1,1,1,32,2048]{4,3,2,1,0:T(8,128)(2,1)S(1)} %copy-done.9, ...), kind=kLoop, calls=%fused_computation.19 | loop fusion | flops 2359296 | bytes 2359296 | tf_op jit(solution)/shard_map/concatenate | solution.py:23
  76.8 3.0 %gather_fusion = bf16[16,16,2048]{2,1,0:T(8,128)(2,1)} fusion(bf16[18,16,2048]{2,1,0:T(8,128)(2,1)} %bitcast.154, s32[1024]{0:T(1024)} %pad_clamp_fusion), kind=kCustom, calls=%fused_computation | custom fusion | bytes 2097216 | tf_op jit(solution)/shard_map/while/body/eval_jaxpr/gather | solution.py:96
  79.8 2.5 %copy.124 = bf16[32,8,16,128]{3,2,1,0:T(8,128)(2,1)} copy(bf16[32,8,16,128]{3,1,2,0:T(8,128)(2,1)} %bitcast.159) | data formatting | bytes 2097152
  85.5 3.6 %collective-permute-start.10 = (bf16[1,3,1,64,2048]{4,3,2,1,0:T(8,128)(2,1)}, bf16[1,3,1,64,2048]{4,3,2,1,0:T(8,128)(2,1)}, u32[]{:S(2)}, u32[]{:S(2)}) collective-permute-start(bf16[1,3,1,64,2048]{4,3,2,1,0:T(8,128)(2,1)} %get-tuple-element.56), channel_id=1, source_target_pairs={{0,1},{1,2},{2,3},{4,5},{5,6},{6,7},{8,9},{9,10},{10,11},{12,13},{... | collective-permute-start | bytes 2359304 | tf_op jit(solution)/shard_map/ppermute | solution.py:19
  89.2 2.3 %pad_maximum_fusion = bf16[1,3,3,32,2048]{4,3,2,1,0:T(8,128)(2,1)} fusion(bf16[1,3,1,32,2048]{4,3,2,1,0:T(8,128)(2,1)} %collective-permute-done.15, bf16[1,1,1,32,2048]{4,3,2,1,0:T(8,128)(2,1)S(1)} %collective-permute-done.13, bf16[1,1,1,32,2048]{4,3,2,1,0:T(8,128)(2,1)S(1)} %bitcast.207, bf16[1,1,1,32,2048]{4,3,2,1,0:T(8,128)(2,1)} %copy-done.10, ...), kind=kLoop, calls=%fused_computation.18 | loop fusion | flops 2359296 | bytes 2359296 | tf_op jit(solution)/shard_map/concatenate | solution.py:23
  91.5 3.0 %gather_fusion.1 = bf16[16,16,2048]{2,1,0:T(8,128)(2,1)} fusion(bf16[18,16,2048]{2,1,0:T(8,128)(2,1)} %bitcast.155, s32[1024]{0:T(1024)} %pad_clamp_fusion), kind=kCustom, calls=%fused_computation.1 | custom fusion | bytes 2097216 | tf_op jit(solution)/shard_map/while/body/eval_jaxpr/gather | solution.py:95
  106.1 2.3 %bitcast_reduce_fusion = (f32[2,16,64]{2,1,0:T(8,128)S(1)}, f32[2,16,704,64]{2,3,1,0:T(8,128)S(1)}) fusion(pred[2,704]{1,0:T(4,128)(4,1)S(1)} %copy-done.12, bf16[2,704,16,128]{3,1,2,0:T(8,128)(2,1)S(1)} %copy_dynamic-update-slice_fusion, bf16[2,64,16,128]{3,2,1,0:T(8,128)(2,1)S(1)} %bitcast.153), kind=kOutput, calls=%fused_computation.3 | convolution fusion | flops 373422080 | bytes 12068224 | tf_op jit(solution)/shard_map/while/body/eval_jaxpr/bqhd,bkhd->bhqk/dot_general | solution.py:102
  112.4 2.2 %fusion.4 = f32[2,64,16,128]{3,1,2,0:T(8,128)S(1)} fusion(bf16[2,704,16,128]{3,1,2,0:T(8,128)(2,1)S(1)} %copy_dynamic-update-slice_fusion.1, f32[2,16,704,64]{2,3,1,0:T(8,128)S(1)} %get-tuple-element.61, f32[2,16,64]{2,1,0:T(8,128)S(1)} %copy_add_fusion, f32[2,16,64]{2,1,0:T(8,128)S(1)} %copy_maximum_fusion, pred[2,704]{1,0:T(4,128)(4,1)S(1)} %copy-done.12), kind=kOutput, calls=%fused_computation.13 | convolution fusion | flops 376307712 | bytes 12600704 | tf_op jit(solution)/shard_map/while/body/eval_jaxpr/bhqk,bkhd->bqhd/dot_general | solution.py:125
  (133 shorter events, 33.3 us)
Async XLA Ops:
  0.0 51.5 %copy-start.4 = (bf16[1,1,2,64,2048]{4,3,2,1,0:T(8,128)(2,1)S(1)}, bf16[1,1,2,64,2048]{4,3,2,1,0:T(8,128)(2,1)}, u32[]{:S(2)}) copy-start(bf16[1,1,2,64,2048]{4,3,2,1,0:T(8,128)(2,1)} %param.10) | copy-start | bytes 1572868
  0.0 48.4 %collective-permute-start = (bf16[1,1,2,64,2048]{4,3,2,1,0:T(8,128)(2,1)}, bf16[1,1,2,64,2048]{4,3,2,1,0:T(8,128)(2,1)S(1)}, u32[]{:S(2)}, u32[]{:S(2)}) collective-permute-start(bf16[1,1,2,64,2048]{4,3,2,1,0:T(8,128)(2,1)} %param.10), channel_id=1, source_target_pairs={{0,4},{4,8},{8,12},{12,16},{16,20},{20,24},{24,28},{1,5},{5,9},{9,... | collective-permute-start | bytes 1572872 | tf_op jit(solution)/shard_map/ppermute | solution.py:19
  3.3 48.2 %collective-permute-start.1 = (bf16[1,1,2,64,2048]{4,3,2,1,0:T(8,128)(2,1)}, bf16[1,1,2,64,2048]{4,3,2,1,0:T(8,128)(2,1)S(1)}, u32[]{:S(2)}, u32[]{:S(2)}) collective-permute-start(bf16[1,1,2,64,2048]{4,3,2,1,0:T(8,128)(2,1)} %param.10), channel_id=1, source_target_pairs={{4,0},{8,4},{12,8},{16,12},{20,16},{24,20},{28,24},{5,1},{9,5},{13... | collective-permute-start | bytes 1572872 | tf_op jit(solution)/shard_map/ppermute | solution.py:22
  5.4 27.2 %collective-permute-start.5 = (bf16[1,1,1,32,2048]{4,3,2,1,0:T(8,128)(2,1)}, bf16[1,1,1,32,2048]{4,3,2,1,0:T(8,128)(2,1)S(1)}, u32[]{:S(2)}, u32[]{:S(2)}) collective-permute-start(bf16[1,1,1,32,2048]{4,3,2,1,0:T(8,128)(2,1)} %bitcast.200), channel_id=1, source_target_pairs={{4,0},{8,4},{12,8},{16,12},{20,16},{24,20},{28,24},{5,1},{9,5},{13... | collective-permute-start | bytes 393224 | tf_op jit(solution)/shard_map/ppermute | solution.py:22
  7.4 29.8 %collective-permute-start.4 = (bf16[1,1,1,32,2048]{4,3,2,1,0:T(8,128)(2,1)}, bf16[1,1,1,32,2048]{4,3,2,1,0:T(8,128)(2,1)S(1)}, u32[]{:S(2)}, u32[]{:S(2)}) collective-permute-start(bf16[1,1,1,32,2048]{4,3,2,1,0:T(8,128)(2,1)} %bitcast.201), channel_id=1, source_target_pairs={{0,4},{4,8},{8,12},{12,16},{16,20},{20,24},{24,28},{1,5},{5,9},{9,... | collective-permute-start | bytes 393224 | tf_op jit(solution)/shard_map/ppermute | solution.py:19
  11.6 28.7 %collective-permute-start.13 = (bf16[1,1,1,32,2048]{4,3,2,1,0:T(8,128)(2,1)}, bf16[1,1,1,32,2048]{4,3,2,1,0:T(8,128)(2,1)S(1)}, u32[]{:S(2)}, u32[]{:S(2)}) collective-permute-start(bf16[1,1,1,32,2048]{4,3,2,1,0:T(8,128)(2,1)} %bitcast.204), channel_id=1, source_target_pairs={{4,0},{8,4},{12,8},{16,12},{20,16},{24,20},{28,24},{5,1},{9,5},{13... | collective-permute-start | bytes 393224 | tf_op jit(solution)/shard_map/ppermute | solution.py:22
  16.2 7.3 %copy-start = (bf16[16,8,16,128]{3,2,1,0:T(8,128)(2,1)}, bf16[16,8,16,128]{3,2,1,0:T(8,128)(2,1)S(1)}, u32[]{:S(2)}) copy-start(bf16[16,8,16,128]{3,2,1,0:T(8,128)(2,1)S(1)} %copy.113) | copy-start | bytes 1572868
  23.5 51.2 %copy-start.5 = (bf16[2,16,2048]{2,1,0:T(8,128)(2,1)S(1)}, bf16[2,16,2048]{2,1,0:T(8,128)(2,1)}, u32[]{:S(2)}) copy-start(bf16[2,16,2048]{2,1,0:T(8,128)(2,1)} %param.12) | copy-start | bytes 393220
  32.6 35.2 %copy-start.7 = (bf16[1,1,1,32,2048]{4,3,2,1,0:T(8,128)(2,1)}, bf16[1,1,1,32,2048]{4,3,2,1,0:T(8,128)(2,1)S(1)}, u32[]{:S(2)}) copy-start(bf16[1,1,1,32,2048]{4,3,2,1,0:T(8,128)(2,1)S(1)} %collective-permute-done.5) | copy-start | bytes 393220
  32.6 10.9 %collective-permute-start.12 = (bf16[1,1,1,32,2048]{4,3,2,1,0:T(8,128)(2,1)}, bf16[1,1,1,32,2048]{4,3,2,1,0:T(8,128)(2,1)S(1)}, u32[]{:S(2)}, u32[]{:S(2)}) collective-permute-start(bf16[1,1,1,32,2048]{4,3,2,1,0:T(8,128)(2,1)} %bitcast.205), channel_id=1, source_target_pairs={{0,4},{4,8},{8,12},{12,16},{16,20},{20,24},{24,28},{1,5},{5,9},{9,... | collective-permute-start | bytes 393224 | tf_op jit(solution)/shard_map/ppermute | solution.py:19
  37.2 11.2 %copy-start.8 = (bf16[1,1,1,32,2048]{4,3,2,1,0:T(8,128)(2,1)}, bf16[1,1,1,32,2048]{4,3,2,1,0:T(8,128)(2,1)S(1)}, u32[]{:S(2)}) copy-start(bf16[1,1,1,32,2048]{4,3,2,1,0:T(8,128)(2,1)S(1)} %collective-permute-done.4) | copy-start | bytes 393220
  37.2 26.1 %collective-permute-start.8 = (bf16[1,1,2,64,2048]{4,3,2,1,0:T(8,128)(2,1)}, bf16[1,1,2,64,2048]{4,3,2,1,0:T(8,128)(2,1)S(1)}, u32[]{:S(2)}, u32[]{:S(2)}) collective-permute-start(bf16[1,1,2,64,2048]{4,3,2,1,0:T(8,128)(2,1)} %param.9), channel_id=1, source_target_pairs={{0,4},{4,8},{8,12},{12,16},{16,20},{20,24},{24,28},{1,5},{5,9},{9,... | collective-permute-start | bytes 1572872 | tf_op jit(solution)/shard_map/ppermute | solution.py:19
  40.4 36.4 %collective-permute-start.9 = (bf16[1,1,2,64,2048]{4,3,2,1,0:T(8,128)(2,1)}, bf16[1,1,2,64,2048]{4,3,2,1,0:T(8,128)(2,1)S(1)}, u32[]{:S(2)}, u32[]{:S(2)}) collective-permute-start(bf16[1,1,2,64,2048]{4,3,2,1,0:T(8,128)(2,1)} %param.9), channel_id=1, source_target_pairs={{4,0},{8,4},{12,8},{16,12},{20,16},{24,20},{28,24},{5,1},{9,5},{13... | collective-permute-start | bytes 1572872 | tf_op jit(solution)/shard_map/ppermute | solution.py:22
  43.5 4.9 %copy-start.10 = (bf16[1,1,1,32,2048]{4,3,2,1,0:T(8,128)(2,1)}, bf16[1,1,1,32,2048]{4,3,2,1,0:T(8,128)(2,1)S(1)}, u32[]{:S(2)}) copy-start(bf16[1,1,1,32,2048]{4,3,2,1,0:T(8,128)(2,1)S(1)} %collective-permute-done.12) | copy-start | bytes 393220
  43.5 25.6 %collective-permute-start.7 = (bf16[1,3,1,32,2048]{4,3,2,1,0:T(8,128)(2,1)S(1)}, bf16[1,3,1,32,2048]{4,3,2,1,0:T(8,128)(2,1)S(1)}, u32[]{:S(2)}, u32[]{:S(2)}) collective-permute-start(bf16[1,3,1,32,2048]{4,3,2,1,0:T(8,128)(2,1)S(1)} %pad_maximum_fusion.3), channel_id=1, source_target_pairs={{1,0},{2,1},{3,2},{5,4},{6,5},{7,6},{9,8},{10,9},{11,10},{13,12},{... | collective-permute-start | bytes 1179656 | tf_op jit(solution)/shard_map/ppermute | solution.py:22
  48.4 22.6 %collective-permute-start.6 = (bf16[1,3,1,32,2048]{4,3,2,1,0:T(8,128)(2,1)S(1)}, bf16[1,3,1,32,2048]{4,3,2,1,0:T(8,128)(2,1)S(1)}, u32[]{:S(2)}, u32[]{:S(2)}) collective-permute-start(bf16[1,3,1,32,2048]{4,3,2,1,0:T(8,128)(2,1)S(1)} %pad_maximum_fusion.3), channel_id=1, source_target_pairs={{0,1},{1,2},{2,3},{4,5},{5,6},{6,7},{8,9},{9,10},{10,11},{12,13},{... | collective-permute-start | bytes 1179656 | tf_op jit(solution)/shard_map/ppermute | solution.py:19
  51.4 23.3 %copy-start.9 = (bf16[1,1,1,32,2048]{4,3,2,1,0:T(8,128)(2,1)S(1)}, bf16[1,1,1,32,2048]{4,3,2,1,0:T(8,128)(2,1)}, u32[]{:S(2)}) copy-start(bf16[1,1,1,32,2048]{4,3,2,1,0:T(8,128)(2,1)} %copy-done.8) | copy-start | bytes 393220
  51.5 34.0 %collective-permute-start.15 = (bf16[1,3,1,32,2048]{4,3,2,1,0:T(8,128)(2,1)}, bf16[1,3,1,32,2048]{4,3,2,1,0:T(8,128)(2,1)}, u32[]{:S(2)}, u32[]{:S(2)}) collective-permute-start(bf16[1,3,1,32,2048]{4,3,2,1,0:T(8,128)(2,1)} %pad_maximum_fusion.2), channel_id=1, source_target_pairs={{1,0},{2,1},{3,2},{5,4},{6,5},{7,6},{9,8},{10,9},{11,10},{13,12},{... | collective-permute-start | bytes 1179656 | tf_op jit(solution)/shard_map/ppermute | solution.py:22
  63.3 25.8 %collective-permute-start.14 = (bf16[1,3,1,32,2048]{4,3,2,1,0:T(8,128)(2,1)}, bf16[1,3,1,32,2048]{4,3,2,1,0:T(8,128)(2,1)}, u32[]{:S(2)}, u32[]{:S(2)}) collective-permute-start(bf16[1,3,1,32,2048]{4,3,2,1,0:T(8,128)(2,1)} %pad_maximum_fusion.2), channel_id=1, source_target_pairs={{0,1},{1,2},{2,3},{4,5},{5,6},{6,7},{8,9},{9,10},{10,11},{12,13},{... | collective-permute-start | bytes 1179656 | tf_op jit(solution)/shard_map/ppermute | solution.py:19
  67.9 21.2 %copy-start.6 = (bf16[2,16,2048]{2,1,0:T(8,128)(2,1)S(1)}, bf16[2,16,2048]{2,1,0:T(8,128)(2,1)}, u32[]{:S(2)}) copy-start(bf16[2,16,2048]{2,1,0:T(8,128)(2,1)} %param.11) | copy-start | bytes 393220
  69.1 26.9 %collective-permute-start.3 = (bf16[1,3,1,64,2048]{4,3,2,1,0:T(8,128)(2,1)}, bf16[1,3,1,64,2048]{4,3,2,1,0:T(8,128)(2,1)}, u32[]{:S(2)}, u32[]{:S(2)}) collective-permute-start(bf16[1,3,1,64,2048]{4,3,2,1,0:T(8,128)(2,1)} %get-tuple-element.59), channel_id=1, source_target_pairs={{1,0},{2,1},{3,2},{5,4},{6,5},{7,6},{9,8},{10,9},{11,10},{13,12},{... | collective-permute-start | bytes 2359304 | tf_op jit(solution)/shard_map/ppermute | solution.py:22
  71.0 24.9 %collective-permute-start.2 = (bf16[1,3,1,64,2048]{4,3,2,1,0:T(8,128)(2,1)}, bf16[1,3,1,64,2048]{4,3,2,1,0:T(8,128)(2,1)}, u32[]{:S(2)}, u32[]{:S(2)}) collective-permute-start(bf16[1,3,1,64,2048]{4,3,2,1,0:T(8,128)(2,1)} %get-tuple-element.58), channel_id=1, source_target_pairs={{0,1},{1,2},{2,3},{4,5},{5,6},{6,7},{8,9},{9,10},{10,11},{12,13},{... | collective-permute-start | bytes 2359304 | tf_op jit(solution)/shard_map/ppermute | solution.py:19
  83.6 17.0 %collective-permute-start.11 = (bf16[1,3,1,64,2048]{4,3,2,1,0:T(8,128)(2,1)}, bf16[1,3,1,64,2048]{4,3,2,1,0:T(8,128)(2,1)}, u32[]{:S(2)}, u32[]{:S(2)}) collective-permute-start(bf16[1,3,1,64,2048]{4,3,2,1,0:T(8,128)(2,1)} %get-tuple-element.57), channel_id=1, source_target_pairs={{1,0},{2,1},{3,2},{5,4},{6,5},{7,6},{9,8},{10,9},{11,10},{13,12},{... | collective-permute-start | bytes 2359304 | tf_op jit(solution)/shard_map/ppermute | solution.py:22
  85.5 15.1 %collective-permute-start.10 = (bf16[1,3,1,64,2048]{4,3,2,1,0:T(8,128)(2,1)}, bf16[1,3,1,64,2048]{4,3,2,1,0:T(8,128)(2,1)}, u32[]{:S(2)}, u32[]{:S(2)}) collective-permute-start(bf16[1,3,1,64,2048]{4,3,2,1,0:T(8,128)(2,1)} %get-tuple-element.56), channel_id=1, source_target_pairs={{0,1},{1,2},{2,3},{4,5},{5,6},{6,7},{8,9},{9,10},{10,11},{12,13},{... | collective-permute-start | bytes 2359304 | tf_op jit(solution)/shard_map/ppermute | solution.py:19
  (7 other events, 19.0 us)
where the time goes:
time: 117 us; the launch traced here: 116 us
  starting transfers between devices  47.1 us (40%)
  local copies, waits for them, and re-layouts  26.6 us (23%)
  other arithmetic  13.9 us (12%)
  blocking collectives  12.9 us (11%)
  waiting for transfers between devices  8.63 us (7%)
  matrix products  6.33 us (5%)
    ppermute x8, starting transfers between devices, extended(): lax.ppermute(lax.slice_in_dim(block, block.shape[dim] - width, None, axis...  29.1 us
    ppermute x8, starting transfers between devices, extended(): lax.ppermute(lax.slice_in_dim(block, 0, width, axis=dim), axis, backward)  18 us
    unnamed x75, local copies, waits for them, and re-layouts  13 us
    ppermute x8, waiting for transfers between devices, extended(): lax.ppermute(lax.slice_in_dim(block, block.shape[dim] - width, None, axis...  8.61 us
    all_gather x1, blocking collectives, body(): lax.all_gather(top_keys, 'col', axis=1, tiled=True)  7.27 us
    concatenate x4, other arithmetic, extended(): block = jnp.concatenate([low, block, high], axis=dim)  7.05 us
    all_gather x1, blocking collectives, body(): lax.all_gather(top_values, 'col', axis=1, tiled=True)  5.64 us
    squeeze x2, other arithmetic, body(): lax.map(attend_image, (queries, near_keys, near_values, local_slot, top_a...  3.46 us
  transfers between devices with their start and end apart: 16, of which 1 were waited for; matrix products, arithmetic and copies ran while one was open for 27% of the time, Pallas kernels for 0%

commit v1 on v0

v1 whole, which is shorter than its diff:
```python
import functools
import math

import jax
import jax.numpy as jnp
from jax import lax
from jax.experimental import pallas as pl
from jax.experimental.pallas import tpu as pltpu
from jax.sharding import PartitionSpec as P

HEADS = 16
NEG_FILL = -1e30
HEADS_PER_CHUNK = 2
AHEAD = 2
OWN, NEAR, FAR = 0, 1, 2


def kernel(
    dims,
    q_in,
    k_in,
    v_in,
    pk_in,
    pv_in,
    tk_in,
    tv_in,
    ids,
    out,
    own,
    left,
    right,
    q_buf,
    out_buf,
    top,
    bias,
    load_sem,
    q_sem,
    out_sem,
    near_send,
    near_recv,
    far_send,
    far_recv,
    left_send,
    left_recv,
    right_send,
    right_recv,
    top_send,
    top_recv,
):
    rows, cols, tokens, pool_rows, pool_blocks, chunks, width, head_width = dims
    pool_tokens = pool_rows // pool_blocks
    r = lax.axis_index("row")
    c = lax.axis_index("col")
    odd = lax.rem(r, 2)
    near_row = r + 1 - 2 * odd
    far_row = r - 1 + 2 * odd
    far_to = r + 2 - 4 * odd
    has_far = (far_row >= 0) & (far_row < rows)
    has_to = (far_to >= 0) & (far_to < rows)
    has_left = c > 0
    has_right = c < cols - 1
    low = 2 * tokens
    mid = low + 2 * pool_rows
    full = mid + 2 * tokens
    edge = mid

    def lanes(g):
        return pl.ds(pl.multiple_of(g * width, width), width)

    def load_chunk(g, _):
        at = lanes(g)
        pieces = (
            (k_in.at[0, 0, 0, :, at], 0, tokens),
            (v_in.at[0, 0, 0, :, at], tokens, tokens),
            (k_in.at[0, 0, 1, :, at], mid, tokens),
            (v_in.at[0, 0, 1, :, at], mid + tokens, tokens),
        )
        for source, start, size in pieces:
            pltpu.make_async_copy(
                source, own.at[OWN, g, pl.ds(start, size)], load_sem.at[g]
            ).start()
        for block in range(pool_blocks):
            for source, start in ((pk_in, low), (pv_in, low + pool_rows)):
                pltpu.make_async_copy(
                    source.at[block, :, at],
                    own.at[OWN, g, pl.ds(start + block * pool_tokens, pool_tokens)],
                    load_sem.at[g],
                ).start()
        return 0

    barrier = pltpu.get_barrier_semaphore()

    def greet(there, row, col):
        @pl.when(there)
        def _():
            pl.semaphore_signal(
                barrier, inc=1, device_id=(row, col), device_id_type=pl.DeviceIdType.MESH
            )

    pl.semaphore_signal(
        barrier, inc=1, device_id=(near_row, c), device_id_type=pl.DeviceIdType.MESH
    )
    greet(r + 2 < rows, r + 2, c)
    greet(r >= 2, r - 2, c)
    for step in range(1, cols):
        pl.semaphore_signal(
            barrier,
            inc=1,
            device_id=(r, lax.rem(c + step, cols)),
            device_id_type=pl.DeviceIdType.MESH,
        )

    lax.fori_loop(0, chunks, load_chunk, 0)
    q_copy = pltpu.make_async_copy(q_in.at[0, 0], q_buf, q_sem)
    q_copy.start()

    top[c] = jnp.concatenate(
        [tk_in[0].astype(jnp.float32), tv_in[0].astype(jnp.float32)], axis=0
    ).astype(jnp.bfloat16)

    @pl.when(jnp.logical_not(has_far))
    def _():
        own[FAR] = jnp.zeros(own.shape[1:], own.dtype)

    @pl.when(jnp.logical_not(has_far & has_left))
    def _():
        left[FAR] = jnp.zeros(left.shape[1:], left.dtype)

    @pl.when(jnp.logical_not(has_far & has_right))
    def _():
        right[FAR] = jnp.zeros(right.shape[1:], right.dtype)

    @pl.when(jnp.logical_not(has_left))
    def _():
        for k in (OWN, NEAR):
            left[k] = jnp.zeros(left.shape[1:], left.dtype)

    @pl.when(jnp.logical_not(has_right))
    def _():
        for k in (OWN, NEAR):
            right[k] = jnp.zeros(right.shape[1:], right.dtype)

    top_rows = cols * tk_in.shape[1]
    for b in range(2):
        parts = []
        for k, row in ((OWN, r), (NEAR, near_row), (FAR, far_row)):
            row_there = (row >= 0) & (row < rows)
            for slot in range(4):
                if slot in (b, b + 1, b + 2):
                    there = row_there
                    if slot == 0:
                        there = there & has_left
                    if slot == 3:
                        there = there & has_right
                    value = jnp.where(there, 0.0, NEG_FILL)
                else:
                    value = jnp.float32(NEG_FILL)
                parts.append(jnp.full((1, tokens), value, jnp.float32))
            for shift in (-1, 0, 1):
                there = row_there & (c + shift >= 0) & (c + shift < cols)
                base = (row * cols + c + shift) * pool_blocks
                for block in range(pool_blocks):
                    listed_here = jnp.int32(0)
                    for n in range(ids.shape[3]):
                        listed_here = listed_here | (ids[0, 0, b, n] == base + block).astype(
                            jnp.int32
                        )
                    listed_here = listed_here * there.astype(jnp.int32)
                    value = (1.0 - listed_here.astype(jnp.float32)) * NEG_FILL
                    parts.append(jnp.full((1, pool_tokens), value, jnp.float32))
        parts.append(jnp.zeros((1, top_rows), jnp.float32))
        at = 0
        for part in parts:
            bias[b : b + 1, at : at + part.shape[1]] = part
            at += part.shape[1]

    greeted = (
        1
        + (r + 2 < rows).astype(jnp.int32)
        + (r >= 2).astype(jnp.int32)
        + (cols - 1)
    )
    pl.semaphore_wait(barrier, greeted)

    def remote(source, target, send, recv, row, col):
        return pltpu.make_async_remote_copy(
            src_ref=source,
            dst_ref=target,
            send_sem=send,
            recv_sem=recv,
            device_id=(row, col),
            device_id_type=pl.DeviceIdType.MESH,
        )

    def near_copy(g):
        return remote(
            own.at[OWN, g], own.at[NEAR, g], near_send, near_recv.at[g], near_row, c
        )

    def far_copy(g):
        return remote(own.at[NEAR, g], own.at[FAR, g], far_send, far_recv.at[g], far_to, c)

    def to_left(k, g):
        return remote(
            own.at[k, g, pl.ds(0, edge)],
            right.at[k, g],
            left_send.at[k],
            right_recv.at[k, g],
            r,
            c - 1,
        )

    def to_right(k, g):
        return remote(
            own.at[k, g, pl.ds(full - edge, edge)],
            left.at[k, g],
            right_send.at[k],
            left_recv.at[k, g],
            r,
            c + 1,
        )

    def sideways(k, g):
        @pl.when(has_left)
        def _():
            to_left(k, g).start()

        @pl.when(has_right)
        def _():
            to_right(k, g).start()

    def top_copy(step):
        to = lax.rem(c + step, cols)
        return remote(top.at[c], top.at[c], top_send.at[step], top_recv.at[step], r, to)

    def send_own(g):
        pltpu.make_async_copy(own.at[OWN, g], own.at[OWN, g], load_sem.at[g]).wait()
        near_copy(g).start()
        sideways(OWN, g)

    send_own(0)
    for step in range(1, cols):
        top_copy(step).start()
    for g in range(1, min(AHEAD, chunks)):
        send_own(g)
    q_copy.wait()

    score_scale = math.log2(math.e) / math.sqrt(head_width)

    def attend(g):
        at = lanes(g)
        q_chunk = q_buf[:, :, at].reshape(2 * tokens, width)
        tops = top[:, :, at].astype(jnp.float32)
        per = tk_in.shape[1]
        top_k = tops[:, :per].reshape(top_rows, width).astype(jnp.bfloat16)
        top_v = tops[:, per:].reshape(top_rows, width).astype(jnp.bfloat16)

        def listed(head, value, top_part):
            lane = pl.ds(head * head_width, head_width)
            fine = tokens if value else 0
            pool = pool_rows if value else 0
            side = full - edge
            parts = []
            for k in (OWN, NEAR, FAR):
                parts += [
                    left[k, g, pl.ds(mid + fine - side, tokens), lane],
                    own[k, g, pl.ds(fine, tokens), lane],
                    own[k, g, pl.ds(mid + fine, tokens), lane],
                    right[k, g, pl.ds(fine, tokens), lane],
                    left[k, g, pl.ds(low + pool - side, pool_rows), lane],
                    own[k, g, pl.ds(low + pool, pool_rows), lane],
                    right[k, g, pl.ds(low + pool, pool_rows), lane],
                ]
            parts.append(top_part[:, head * head_width : (head + 1) * head_width])
            return jnp.concatenate(parts, axis=0)

        for head in range(width // head_width):
            q_head = q_chunk[:, head * head_width : (head + 1) * head_width]
            scores = lax.dot_general(
                q_head,
                listed(head, False, top_k),
                (((1,), (1,)), ((), ())),
                preferred_element_type=jnp.float32,
            )
            scores = (scores * score_scale).reshape(2, tokens, -1) + bias[...][:, None, :]
            peak = jnp.max(scores, axis=-1, keepdims=True)
            exponent = jnp.exp2(scores - peak)
            total = jnp.sum(exponent, axis=-1, keepdims=True)
            weights = (exponent * (1.0 / total)).astype(jnp.bfloat16)
            result = jnp.dot(
                weights.reshape(2 * tokens, -1),
                listed(head, True, top_v),
                preferred_element_type=jnp.float32,
            )
            out_buf[g, :, :, head * head_width : (head + 1) * head_width] = result.reshape(
                2, tokens, head_width
            ).astype(jnp.bfloat16)
        pltpu.make_async_copy(out_buf.at[g], out.at[0, 0, :, :, at], out_sem).start()

    def step(t, _):
        @pl.when(t < chunks)
        def _():
            near_copy(t).wait_recv()

            @pl.when(has_to)
            def _():
                far_copy(t).start()

            sideways(NEAR, t)

        @pl.when(t + AHEAD < chunks)
        def _():
            send_own(t + AHEAD)

        @pl.when((t >= 1) & (t <= chunks) & has_far)
        def _():
            far_copy(t - 1).wait_recv()
            sideways(FAR, t - 1)

        @pl.when(t >= 2)
        def _():
            g = t - 2

            @pl.when(g == 0)
            def _():
                for s in range(1, cols):
                    top_copy(s).wait_recv()

            @pl.when(has_left)
            def _():
                to_right(OWN, g).wait_recv()
                to_right(NEAR, g).wait_recv()

            @pl.when(has_right)
            def _():
                to_left(OWN, g).wait_recv()
                to_left(NEAR, g).wait_recv()

            @pl.when(has_far & has_left)
            def _():
                to_right(FAR, g).wait_recv()

            @pl.when(has_far & has_right)
            def _():
                to_left(FAR, g).wait_recv()

            attend(g)

        return 0

    lax.fori_loop(0, chunks + 2, step, 0)

    remote(own.at[OWN], own.at[NEAR], near_send, near_recv.at[0], near_row, c).wait_send()

    @pl.when(has_to)
    def _():
        remote(own.at[NEAR], own.at[FAR], far_send, far_recv.at[0], far_to, c).wait_send()

    def sent(k):
        @pl.when(has_left)
        def _():
            remote(
                own.at[k, :, pl.ds(0, edge)],
                right.at[k],
                left_send.at[k],
                right_recv.at[k, 0],
                r,
                c - 1,
            ).wait_send()

        @pl.when(has_right)
        def _():
            remote(
                own.at[k, :, pl.ds(full - edge, edge)],
                left.at[k],
                right_send.at[k],
                left_recv.at[k, 0],
                r,
                c + 1,
            ).wait_send()

    sent(OWN)
    sent(NEAR)

    @pl.when(has_far)
    def _():
        sent(FAR)

    for s in range(1, cols):
        top_copy(s).wait_send()
    pltpu.make_async_copy(out_buf, out_buf, out_sem).wait()


def solution(mesh):
    row_count, col_count = mesh.shape["row"], mesh.shape["col"]

    def body(queries, keys, values, pool_keys, pool_values, top_keys, top_values, coarse_ids):
        tokens, model_width = queries.shape[3:]
        pool_blocks, pool_tokens, _ = pool_keys.shape
        pool_rows = pool_blocks * pool_tokens
        head_width = model_width // HEADS
        width = HEADS_PER_CHUNK * head_width
        chunks = model_width // width
        full = 4 * tokens + 2 * pool_rows
        edge = 2 * tokens + 2 * pool_rows
        per = top_keys.shape[1]
        listed = 3 * (4 * tokens + 3 * pool_rows) + col_count * per
        dims = (row_count, col_count, tokens, pool_rows, pool_blocks, chunks, width, head_width)
        dma = pltpu.SemaphoreType.DMA
        return pl.pallas_call(
            functools.partial(kernel, dims),
            out_shape=jax.ShapeDtypeStruct(queries.shape, queries.dtype),
            in_specs=[pl.BlockSpec(memory_space=pl.ANY)] * 5
            + [pl.BlockSpec(memory_space=pltpu.VMEM)] * 2
            + [pl.BlockSpec(memory_space=pltpu.SMEM)],
            out_specs=pl.BlockSpec(memory_space=pl.ANY),
            scratch_shapes=[
                pltpu.VMEM((3, chunks, full, width), jnp.bfloat16),
                pltpu.VMEM((3, chunks, edge, width), jnp.bfloat16),
                pltpu.VMEM((3, chunks, edge, width), jnp.bfloat16),
                pltpu.VMEM((2, tokens, model_width), jnp.bfloat16),
                pltpu.VMEM((chunks, 2, tokens, width), jnp.bfloat16),
                pltpu.VMEM((col_count, 2 * per, model_width), jnp.bfloat16),
                pltpu.VMEM((2, listed), jnp.float32),
                dma((chunks,)),
                dma,
                dma,
                dma,
                dma((chunks,)),
                dma,
                dma((chunks,)),
                dma((3,)),
                dma((3, chunks)),
                dma((3,)),
                dma((3, chunks)),
                dma((col_count,)),
                dma((col_count,)),
            ],
            compiler_params=pltpu.CompilerParams(
                collective_id=0, has_side_effects=True, vmem_limit_bytes=40 * 2**20
            ),
            cost_estimate=pl.CostEstimate(
                flops=4 * 2 * tokens * listed * model_width,
                bytes_accessed=8 * 2**20,
                transcendentals=2 * tokens * listed * HEADS,
            ),
        )(queries, keys, values, pool_keys, pool_values, top_keys, top_values, coarse_ids)

    placed = (
        P(None, "row", "col", None, None),
        P(None, "row", "col", None, None),
        P(None, "row", "col", None, None),
        P(("row", "col"), None, None),
        P(("row", "col"), None, None),
        P(None, "col", None),
        P(None, "col", None),
        P(None, "row", "col", None),
    )
    return jax.shard_map(
        body,
        mesh=mesh,
        in_specs=placed,
        out_specs=P(None, "row", "col", None, None),
        check_vma=False,
    )
```

time: 117 us -> 52.2 us (0.45)
  starting transfers between devices: 47.1 us -> 0 us
  Pallas kernels: 0 us -> 43.6 us
  local copies, waits for them, and re-layouts: 26.6 us -> 7.92 us
  other arithmetic: 13.9 us -> 0 us
  blocking collectives: 12.9 us -> 0 us
  waiting for transfers between devices: 8.63 us -> 0 us
  matrix products: 6.33 us -> 0 us
    ppermute x16 -> x0, starting transfers between devices: 47.1 us -> none  [the longest x8 29.1 us: extended(): lax.ppermute(lax.slice_in_dim(block, block.shape[dim] - width, None, axis...]
    pallas_call x0 -> x1, Pallas kernels: none -> 43.6 us  [body(): pl.pallas_call(functools.partial(kernel, dims), out_shape=jax.ShapeDtypeS...]
    all_gather x2 -> x0, blocking collectives: 12.9 us -> none  [the longest x1 7.27 us: body(): lax.all_gather(top_keys, 'col', axis=1, tiled=True)]
    ppermute x16 -> x0, waiting for transfers between devices: 8.63 us -> none  [the longest x8 8.61 us: extended(): lax.ppermute(lax.slice_in_dim(block, block.shape[dim] - width, None, axis...]
    concatenate x4 -> x0, other arithmetic: 7.05 us -> none  [extended(): block = jnp.concatenate([low, block, high], axis=dim)]
    dot_general x4 -> x0, matrix products: 6.33 us -> none  [the longest x1 2.34 us: attend_image(): jnp.einsum('bqhd,bkhd->bhqk', query_heads, key_list, preferred_element_ty...]
    gather x2 -> x0, local copies, waits for them, and re-layouts: 5.96 us -> none  [the longest x1 2.98 us: attend_image(): around_values[slot_image].reshape(blocks, coarse_length, model_width)]
    unnamed x75 -> x17, local copies, waits for them, and re-layouts: 13 us -> 7.92 us
  transfers between devices with their start and end apart: 16 -> 0, of which waited for: 1 -> 0; matrix products, arithmetic and copies ran while one was open for 27% -> 0% of each run, Pallas kernels for 0% -> 0%
where the time goes in v1:
time: 52.2 us; the launch traced here: 51.6 us
  Pallas kernels  43.6 us (84%)
  local copies, waits for them, and re-layouts  7.92 us (15%)
    pallas_call x1, Pallas kernels, body(): pl.pallas_call(functools.partial(kernel, dims), out_shape=jax.ShapeDtypeS...  43.6 us
    unnamed x17, local copies, waits for them, and re-layouts  7.92 us

profile of v1, /device:TPU:5, one launch (start us, length us, event | category | flops | bytes accessed | tf_op | source)
XLA Modules:
  0.0 51.6 jit_solution(6495987087461273501)
XLA Ops:
  0.0 0.0 copy-start
  0.0 1.0 %copy-done = bf16[1,1,2,64,2048]{4,3,2,1,0:T(8,128)(2,1)S(1)} copy-done((bf16[1,1,2,64,2048]{4,3,2,1,0:T(8,128)(2,1)S(1)}, bf16[1,1,2,64,2048]{4,3,2,1,0:T(8,128)(2,1)}, u32[]{:S(2)}) %copy-start) | copy-done | bytes 524312
  1.0 0.0 copy-start.1
  1.0 1.0 %copy-done.1 = bf16[1,1,2,64,2048]{4,3,2,1,0:T(8,128)(2,1)S(1)} copy-done((bf16[1,1,2,64,2048]{4,3,2,1,0:T(8,128)(2,1)S(1)}, bf16[1,1,2,64,2048]{4,3,2,1,0:T(8,128)(2,1)}, u32[]{:S(2)}) %copy-start.1) | copy-done | bytes 524312
  2.1 0.0 copy-start.2
  2.1 1.0 %copy-done.2 = bf16[1,1,2,64,2048]{4,3,2,1,0:T(8,128)(2,1)S(1)} copy-done((bf16[1,1,2,64,2048]{4,3,2,1,0:T(8,128)(2,1)S(1)}, bf16[1,1,2,64,2048]{4,3,2,1,0:T(8,128)(2,1)}, u32[]{:S(2)}) %copy-start.2) | copy-done | bytes 524312
  3.1 0.0 copy-start.3
  3.1 0.9 %copy-done.3 = bf16[2,16,2048]{2,1,0:T(8,128)(2,1)S(1)} copy-done((bf16[2,16,2048]{2,1,0:T(8,128)(2,1)S(1)}, bf16[2,16,2048]{2,1,0:T(8,128)(2,1)}, u32[]{:S(2)}) %copy-start.3) | copy-done | bytes 131096
  4.0 0.0 copy-start.4
  4.0 0.9 %copy-done.4 = bf16[2,16,2048]{2,1,0:T(8,128)(2,1)S(1)} copy-done((bf16[2,16,2048]{2,1,0:T(8,128)(2,1)S(1)}, bf16[2,16,2048]{2,1,0:T(8,128)(2,1)}, u32[]{:S(2)}) %copy-start.4) | copy-done | bytes 131096
  4.9 0.0 copy-start.5
  4.9 0.8 %copy-done.5 = bf16[1,8,2048]{2,1,0:T(8,128)(2,1)S(1)} copy-done((bf16[1,8,2048]{2,1,0:T(8,128)(2,1)S(1)}, bf16[1,8,2048]{2,1,0:T(8,128)(2,1)}, u32[]{:S(2)}) %copy-start.5) | copy-done | bytes 32792
  5.7 0.0 copy-start.6
  5.7 0.8 %copy-done.6 = bf16[1,8,2048]{2,1,0:T(8,128)(2,1)S(1)} copy-done((bf16[1,8,2048]{2,1,0:T(8,128)(2,1)S(1)}, bf16[1,8,2048]{2,1,0:T(8,128)(2,1)}, u32[]{:S(2)}) %copy-start.6) | copy-done | bytes 32792
  6.5 0.0 copy-start.7
  6.5 0.7 %copy-done.7 = s32[1,1,2,8]{3,2,1,0:T(2,128)S(1)} copy-done((s32[1,1,2,8]{3,2,1,0:T(2,128)S(1)}, s32[1,1,2,8]{3,2,1,0:T(2,128)}, u32[]{:S(2)}) %copy-start.7) | copy-done | bytes 88
  7.1 43.6 %shard_map.82 = bf16[1,1,2,64,2048]{4,3,2,1,0:T(8,128)(2,1)S(1)} custom-call(bf16[1,1,2,64,2048]{4,3,2,1,0:T(8,128)(2,1)S(1)} %copy-done, bf16[1,1,2,64,2048]{4,3,2,1,0:T(8,128)(2,1)S(1)} %copy-done.1, bf16[1,1,2,64,2048]{4,3,2,1,0:T(8,128)(2,1)S(1)} %copy-done.2, bf16[2,16,2048]{2,1,0:T(8,128)(2,1)S(1)} %copy-done.3, bf16[2,16,2048]{2,1,0:T(8,128)(2,1)S(1)} %copy-done.4, ...), custom_call_target="tpu_custom_call" | custom-call | flops 1140850688 | bytes 8388608 | tf_op jit(solution)/shard_map/pallas_call | solution.py:410
  50.8 0.8 %copy.10 = bf16[1,1,2,64,2048]{4,3,2,1,0:T(8,128)(2,1)} copy(bf16[1,1,2,64,2048]{4,3,2,1,0:T(8,128)(2,1)S(1)} %shard_map.82) | data formatting | bytes 1048576
Async XLA Ops:
  0.0 1.0 %copy-start = (bf16[1,1,2,64,2048]{4,3,2,1,0:T(8,128)(2,1)S(1)}, bf16[1,1,2,64,2048]{4,3,2,1,0:T(8,128)(2,1)}, u32[]{:S(2)}) copy-start(bf16[1,1,2,64,2048]{4,3,2,1,0:T(8,128)(2,1)} %q_in.1) | copy-start | bytes 1572868
  1.0 1.0 %copy-start.1 = (bf16[1,1,2,64,2048]{4,3,2,1,0:T(8,128)(2,1)S(1)}, bf16[1,1,2,64,2048]{4,3,2,1,0:T(8,128)(2,1)}, u32[]{:S(2)}) copy-start(bf16[1,1,2,64,2048]{4,3,2,1,0:T(8,128)(2,1)} %k_in.1) | copy-start | bytes 1572868
  2.1 1.0 %copy-start.2 = (bf16[1,1,2,64,2048]{4,3,2,1,0:T(8,128)(2,1)S(1)}, bf16[1,1,2,64,2048]{4,3,2,1,0:T(8,128)(2,1)}, u32[]{:S(2)}) copy-start(bf16[1,1,2,64,2048]{4,3,2,1,0:T(8,128)(2,1)} %v_in.1) | copy-start | bytes 1572868
  3.1 0.9 %copy-start.3 = (bf16[2,16,2048]{2,1,0:T(8,128)(2,1)S(1)}, bf16[2,16,2048]{2,1,0:T(8,128)(2,1)}, u32[]{:S(2)}) copy-start(bf16[2,16,2048]{2,1,0:T(8,128)(2,1)} %pk_in.1) | copy-start | bytes 393220
  4.0 0.9 %copy-start.4 = (bf16[2,16,2048]{2,1,0:T(8,128)(2,1)S(1)}, bf16[2,16,2048]{2,1,0:T(8,128)(2,1)}, u32[]{:S(2)}) copy-start(bf16[2,16,2048]{2,1,0:T(8,128)(2,1)} %pv_in.1) | copy-start | bytes 393220
  4.9 0.8 %copy-start.5 = (bf16[1,8,2048]{2,1,0:T(8,128)(2,1)S(1)}, bf16[1,8,2048]{2,1,0:T(8,128)(2,1)}, u32[]{:S(2)}) copy-start(bf16[1,8,2048]{2,1,0:T(8,128)(2,1)} %tk_in.1) | copy-start | bytes 98308
  5.7 0.8 %copy-start.6 = (bf16[1,8,2048]{2,1,0:T(8,128)(2,1)S(1)}, bf16[1,8,2048]{2,1,0:T(8,128)(2,1)}, u32[]{:S(2)}) copy-start(bf16[1,8,2048]{2,1,0:T(8,128)(2,1)} %tv_in.1) | copy-start | bytes 98308
  6.5 0.7 %copy-start.7 = (s32[1,1,2,8]{3,2,1,0:T(2,128)S(1)}, s32[1,1,2,8]{3,2,1,0:T(2,128)}, u32[]{:S(2)}) copy-start(s32[1,1,2,8]{3,2,1,0:T(2,128)} %ids.1) | copy-start | bytes 196

commit v2 on v1

--- a/solution.py
+++ b/solution.py
@@ -24,7 +24,7 @@
     pv_in,
     tk_in,
     tv_in,
-    ids,
+    ids_in,
     out,
     own,
     left,
@@ -32,8 +32,12 @@
     q_buf,
     out_buf,
     top,
+    top_own,
+    ids,
     bias,
     load_sem,
+    top_sem,
+    ids_sem,
     q_sem,
     out_sem,
     near_send,
@@ -110,12 +114,21 @@
             device_id_type=pl.DeviceIdType.MESH,
         )
 
+    ids_copy = pltpu.make_async_copy(ids_in, ids, ids_sem)
+    ids_copy.start()
+    tk_copy = pltpu.make_async_copy(tk_in.at[0], top_own.at[0], top_sem.at[0])
+    tk_copy.start()
+    tv_copy = pltpu.make_async_copy(tv_in.at[0], top_own.at[1], top_sem.at[1])
+    tv_copy.start()
     lax.fori_loop(0, chunks, load_chunk, 0)
     q_copy = pltpu.make_async_copy(q_in.at[0, 0], q_buf, q_sem)
     q_copy.start()
 
+    tk_copy.wait()
+    tv_copy.wait()
+    ids_copy.wait()
     top[c] = jnp.concatenate(
-        [tk_in[0].astype(jnp.float32), tv_in[0].astype(jnp.float32)], axis=0
+        [top_own[0].astype(jnp.float32), top_own[1].astype(jnp.float32)], axis=0
     ).astype(jnp.bfloat16)
 
     @pl.when(jnp.logical_not(has_far))
@@ -410,9 +423,7 @@
         return pl.pallas_call(
             functools.partial(kernel, dims),
             out_shape=jax.ShapeDtypeStruct(queries.shape, queries.dtype),
-            in_specs=[pl.BlockSpec(memory_space=pl.ANY)] * 5
-            + [pl.BlockSpec(memory_space=pltpu.VMEM)] * 2
-            + [pl.BlockSpec(memory_space=pltpu.SMEM)],
+            in_specs=[pl.BlockSpec(memory_space=pltpu.HBM)] * 8,
             out_specs=pl.BlockSpec(memory_space=pl.ANY),
             scratch_shapes=[
                 pltpu.VMEM((3, chunks, full, width), jnp.bfloat16),
@@ -421,8 +432,12 @@
                 pltpu.VMEM((2, tokens, model_width), jnp.bfloat16),
                 pltpu.VMEM((chunks, 2, tokens, width), jnp.bfloat16),
                 pltpu.VMEM((col_count, 2 * per, model_width), jnp.bfloat16),
+                pltpu.VMEM((2, per, model_width), jnp.bfloat16),
+                pltpu.SMEM(coarse_ids.shape, jnp.int32),
                 pltpu.VMEM((2, listed), jnp.float32),
                 dma((chunks,)),
+                dma((2,)),
+                dma,
                 dma,
                 dma,
                 dma,
@@ -437,7 +452,7 @@
                 dma((col_count,)),
             ],
             compiler_params=pltpu.CompilerParams(
-                collective_id=0, has_side_effects=True, vmem_limit_bytes=40 * 2**20
+                collective_id=0, has_side_effects=True, vmem_limit_bytes=63 * 2**20
             ),
             cost_estimate=pl.CostEstimate(
                 flops=4 * 2 * tokens * listed * model_width,

time: 52.2 us -> 45.6 us (0.87)
  local copies, waits for them, and re-layouts: 7.92 us -> 1.88 us
    unnamed x17 -> x1, local copies, waits for them, and re-layouts: 7.92 us -> 1.88 us
where the time goes in v2:
time: 45.6 us; the launch traced here: 45.4 us
  Pallas kernels  43.5 us (95%)
  local copies, waits for them, and re-layouts  1.88 us (4%)
    pallas_call x1, Pallas kernels, body(): pl.pallas_call(functools.partial(kernel, dims), out_shape=jax.ShapeDtypeS...  43.5 us
    unnamed x1, local copies, waits for them, and re-layouts  1.88 us

profile of v2, /device:TPU:5, one launch (start us, length us, event | category | flops | bytes accessed | tf_op | source)
XLA Modules:
  0.0 45.4 jit_solution(17816004976582876889)
XLA Ops:
  0.0 43.5 %shard_map.82 = bf16[1,1,2,64,2048]{4,3,2,1,0:T(8,128)(2,1)} custom-call(bf16[1,1,2,64,2048]{4,3,2,1,0:T(8,128)(2,1)} %q_in.1, bf16[1,1,2,64,2048]{4,3,2,1,0:T(8,128)(2,1)} %k_in.1, bf16[1,1,2,64,2048]{4,3,2,1,0:T(8,128)(2,1)} %v_in.1, bf16[2,16,2048]{2,1,0:T(8,128)(2,1)} %pk_in.1, bf16[2,16,2048]{2,1,0:T(8,128)(2,1)} %pv_in.1, bf16[1,8,2048]{2,1,0:T(8,128)(2,1)} %tk_in.1, ...), custom_call_target="tpu_custom_call" | custom-call | flops 1140850688 | bytes 8388608 | tf_op jit(solution)/shard_map/pallas_call | solution.py:423
  43.5 1.9 %copy.10 = bf16[1,1,2,64,2048]{4,3,2,1,0:T(8,128)(2,1)} copy(bf16[1,1,2,64,2048]{4,3,2,1,0:T(8,128)(2,1)} %shard_map.82) | data formatting | bytes 1048576

commit v3 on v2

--- a/solution.py
+++ b/solution.py
@@ -10,7 +10,7 @@
 
 HEADS = 16
 NEG_FILL = -1e30
-HEADS_PER_CHUNK = 2
+HEADS_PER_CHUNK = 1
 AHEAD = 2
 OWN, NEAR, FAR = 0, 1, 2
 

time: 45.6 us -> 53.4 us (1.17)
  Pallas kernels: 43.5 us -> 51.4 us
    pallas_call x1, Pallas kernels: 43.5 us -> 51.4 us  [body(): pl.pallas_call(functools.partial(kernel, dims), out_shape=jax.ShapeDtypeS...]
where the time goes in v3:
time: 53.4 us; the launch traced here: 53.3 us
  Pallas kernels  51.4 us (96%)
  local copies, waits for them, and re-layouts  1.88 us (4%)
    pallas_call x1, Pallas kernels, body(): pl.pallas_call(functools.partial(kernel, dims), out_shape=jax.ShapeDtypeS...  51.4 us
    unnamed x1, local copies, waits for them, and re-layouts  1.88 us

profile of v3, /device:TPU:5, one launch (start us, length us, event | category | flops | bytes accessed | tf_op | source)
XLA Modules:
  0.0 53.3 jit_solution(17508545845395308377)
XLA Ops:
  0.0 51.4 %shard_map.82 = bf16[1,1,2,64,2048]{4,3,2,1,0:T(8,128)(2,1)} custom-call(bf16[1,1,2,64,2048]{4,3,2,1,0:T(8,128)(2,1)} %q_in.1, bf16[1,1,2,64,2048]{4,3,2,1,0:T(8,128)(2,1)} %k_in.1, bf16[1,1,2,64,2048]{4,3,2,1,0:T(8,128)(2,1)} %v_in.1, bf16[2,16,2048]{2,1,0:T(8,128)(2,1)} %pk_in.1, bf16[2,16,2048]{2,1,0:T(8,128)(2,1)} %pv_in.1, bf16[1,8,2048]{2,1,0:T(8,128)(2,1)} %tk_in.1, ...), custom_call_target="tpu_custom_call" | custom-call | flops 1140850688 | bytes 8388608 | tf_op jit(solution)/shard_map/pallas_call | solution.py:423
  51.4 1.9 %copy.10 = bf16[1,1,2,64,2048]{4,3,2,1,0:T(8,128)(2,1)} copy(bf16[1,1,2,64,2048]{4,3,2,1,0:T(8,128)(2,1)} %shard_map.82) | data formatting | bytes 1048576

commit v4 on v3

--- a/solution.py
+++ b/solution.py
@@ -11,7 +11,10 @@
 HEADS = 16
 NEG_FILL = -1e30
 HEADS_PER_CHUNK = 1
-AHEAD = 2
+AHEAD = 3
+LOADS = 6
+FAR_LAG = 2
+ATTEND_LAG = 3
 OWN, NEAR, FAR = 0, 1, 2
 
 
@@ -78,18 +81,13 @@
             (v_in.at[0, 0, 0, :, at], tokens, tokens),
             (k_in.at[0, 0, 1, :, at], mid, tokens),
             (v_in.at[0, 0, 1, :, at], mid + tokens, tokens),
+            (pk_in.at[:, at], low, pool_rows),
+            (pv_in.at[:, at], low + pool_rows, pool_rows),
         )
         for source, start, size in pieces:
             pltpu.make_async_copy(
                 source, own.at[OWN, g, pl.ds(start, size)], load_sem.at[g]
             ).start()
-        for block in range(pool_blocks):
-            for source, start in ((pk_in, low), (pv_in, low + pool_rows)):
-                pltpu.make_async_copy(
-                    source.at[block, :, at],
-                    own.at[OWN, g, pl.ds(start + block * pool_tokens, pool_tokens)],
-                    load_sem.at[g],
-                ).start()
         return 0
 
     barrier = pltpu.get_barrier_semaphore()
@@ -114,22 +112,91 @@
             device_id_type=pl.DeviceIdType.MESH,
         )
 
+    lax.fori_loop(0, min(LOADS, chunks), load_chunk, 0)
     ids_copy = pltpu.make_async_copy(ids_in, ids, ids_sem)
     ids_copy.start()
     tk_copy = pltpu.make_async_copy(tk_in.at[0], top_own.at[0], top_sem.at[0])
     tk_copy.start()
     tv_copy = pltpu.make_async_copy(tv_in.at[0], top_own.at[1], top_sem.at[1])
     tv_copy.start()
-    lax.fori_loop(0, chunks, load_chunk, 0)
     q_copy = pltpu.make_async_copy(q_in.at[0, 0], q_buf, q_sem)
     q_copy.start()
 
+    greeted = (
+        1
+        + (r + 2 < rows).astype(jnp.int32)
+        + (r >= 2).astype(jnp.int32)
+        + (cols - 1)
+    )
+    pl.semaphore_wait(barrier, greeted)
+
+    def remote(source, target, send, recv, row, col):
+        return pltpu.make_async_remote_copy(
+            src_ref=source,
+            dst_ref=target,
+            send_sem=send,
+            recv_sem=recv,
+            device_id=(row, col),
+            device_id_type=pl.DeviceIdType.MESH,
+        )
+
+    def near_copy(g):
+        return remote(
+            own.at[OWN, g], own.at[NEAR, g], near_send, near_recv.at[g], near_row, c
+        )
+
+    def far_copy(g):
+        return remote(own.at[NEAR, g], own.at[FAR, g], far_send, far_recv.at[g], far_to, c)
+
+    def to_left(k, g):
+        return remote(
+            own.at[k, g, pl.ds(0, edge)],
+            right.at[k, g],
+            left_send.at[k],
+            right_recv.at[k, g],
+            r,
+            c - 1,
+        )
+
+    def to_right(k, g):
+        return remote(
+            own.at[k, g, pl.ds(full - edge, edge)],
+            left.at[k, g],
+            right_send.at[k],
+            left_recv.at[k, g],
+            r,
+            c + 1,
+        )
+
+    def sideways(k, g):
+        @pl.when(has_left)
+        def _():
+            to_left(k, g).start()
+
+        @pl.when(has_right)
+        def _():
+            to_right(k, g).start()
+
+    def top_copy(step):
+        to = lax.rem(c + step, cols)
+        return remote(top.at[c], top.at[c], top_send.at[step], top_recv.at[step], r, to)
+
+    def send_own(g):
+        pltpu.make_async_copy(own.at[OWN, g], own.at[OWN, g], load_sem.at[g]).wait()
+        near_copy(g).start()
+        sideways(OWN, g)
+
+    for g in range(min(AHEAD, chunks)):
+        send_own(g)
     tk_copy.wait()
     tv_copy.wait()
     ids_copy.wait()
     top[c] = jnp.concatenate(
         [top_own[0].astype(jnp.float32), top_own[1].astype(jnp.float32)], axis=0
     ).astype(jnp.bfloat16)
+
+    for step in range(1, cols):
+        top_copy(step).start()
 
     @pl.when(jnp.logical_not(has_far))
     def _():
@@ -187,75 +254,6 @@
             bias[b : b + 1, at : at + part.shape[1]] = part
             at += part.shape[1]
 
-    greeted = (
-        1
-        + (r + 2 < rows).astype(jnp.int32)
-        + (r >= 2).astype(jnp.int32)
-        + (cols - 1)
-    )
-    pl.semaphore_wait(barrier, greeted)
-
-    def remote(source, target, send, recv, row, col):
-        return pltpu.make_async_remote_copy(
-            src_ref=source,
-            dst_ref=target,
-            send_sem=send,
-            recv_sem=recv,
-            device_id=(row, col),
-            device_id_type=pl.DeviceIdType.MESH,
-        )
-
-    def near_copy(g):
-        return remote(
-            own.at[OWN, g], own.at[NEAR, g], near_send, near_recv.at[g], near_row, c
-        )
-
-    def far_copy(g):
-        return remote(own.at[NEAR, g], own.at[FAR, g], far_send, far_recv.at[g], far_to, c)
-
-    def to_left(k, g):
-        return remote(
-            own.at[k, g, pl.ds(0, edge)],
-            right.at[k, g],
-            left_send.at[k],
-            right_recv.at[k, g],
-            r,
-            c - 1,
-        )
-
-    def to_right(k, g):
-        return remote(
-            own.at[k, g, pl.ds(full - edge, edge)],
-            left.at[k, g],
-            right_send.at[k],
-            left_recv.at[k, g],
-            r,
-            c + 1,
-        )
-
-    def sideways(k, g):
-        @pl.when(has_left)
-        def _():
-            to_left(k, g).start()
-
-        @pl.when(has_right)
-        def _():
-            to_right(k, g).start()
-
-    def top_copy(step):
-        to = lax.rem(c + step, cols)
-        return remote(top.at[c], top.at[c], top_send.at[step], top_recv.at[step], r, to)
-
-    def send_own(g):
-        pltpu.make_async_copy(own.at[OWN, g], own.at[OWN, g], load_sem.at[g]).wait()
-        near_copy(g).start()
-        sideways(OWN, g)
-
-    send_own(0)
-    for step in range(1, cols):
-        top_copy(step).start()
-    for g in range(1, min(AHEAD, chunks)):
-        send_own(g)
     q_copy.wait()
 
     score_scale = math.log2(math.e) / math.sqrt(head_width)
@@ -325,14 +323,18 @@
         def _():
             send_own(t + AHEAD)
 
-        @pl.when((t >= 1) & (t <= chunks) & has_far)
-        def _():
-            far_copy(t - 1).wait_recv()
-            sideways(FAR, t - 1)
-
-        @pl.when(t >= 2)
-        def _():
-            g = t - 2
+        @pl.when(t + LOADS < chunks)
+        def _():
+            load_chunk(t + LOADS, 0)
+
+        @pl.when((t >= FAR_LAG) & (t < chunks + FAR_LAG) & has_far)
+        def _():
+            far_copy(t - FAR_LAG).wait_recv()
+            sideways(FAR, t - FAR_LAG)
+
+        @pl.when(t >= ATTEND_LAG)
+        def _():
+            g = t - ATTEND_LAG
 
             @pl.when(g == 0)
             def _():
@@ -361,7 +363,7 @@
 
         return 0
 
-    lax.fori_loop(0, chunks + 2, step, 0)
+    lax.fori_loop(0, chunks + ATTEND_LAG, step, 0)
 
     remote(own.at[OWN], own.at[NEAR], near_send, near_recv.at[0], near_row, c).wait_send()
 
@@ -459,7 +461,16 @@
                 bytes_accessed=8 * 2**20,
                 transcendentals=2 * tokens * listed * HEADS,
             ),
-        )(queries, keys, values, pool_keys, pool_values, top_keys, top_values, coarse_ids)
+        )(
+            queries,
+            keys,
+            values,
+            pool_keys.reshape(pool_rows, model_width),
+            pool_values.reshape(pool_rows, model_width),
+            top_keys,
+            top_values,
+            coarse_ids,
+        )
 
     placed = (
         P(None, "row", "col", None, None),

time: 53.4 us -> 49.7 us (0.931)
  Pallas kernels: 51.4 us -> 47.6 us
    pallas_call x1, Pallas kernels: 51.4 us -> 47.6 us  [body(): pl.pallas_call(functools.partial(kernel, dims), out_shape=jax.ShapeDtypeS...]
where the time goes in v4:
time: 49.7 us; the launch traced here: 49.5 us
  Pallas kernels  47.6 us (96%)
  local copies, waits for them, and re-layouts  1.88 us (4%)
    pallas_call x1, Pallas kernels, body(): pl.pallas_call(functools.partial(kernel, dims), out_shape=jax.ShapeDtypeS...  47.6 us
    unnamed x1, local copies, waits for them, and re-layouts  1.88 us

profile of v4, /device:TPU:5, one launch (start us, length us, event | category | flops | bytes accessed | tf_op | source)
XLA Modules:
  0.0 49.5 jit_solution(6534977354780926766)
XLA Ops:
  0.0 47.6 %shard_map.82 = bf16[1,1,2,64,2048]{4,3,2,1,0:T(8,128)(2,1)} custom-call(bf16[1,1,2,64,2048]{4,3,2,1,0:T(8,128)(2,1)} %q_in.1, bf16[1,1,2,64,2048]{4,3,2,1,0:T(8,128)(2,1)} %k_in.1, bf16[1,1,2,64,2048]{4,3,2,1,0:T(8,128)(2,1)} %v_in.1, bf16[32,2048]{1,0:T(8,128)(2,1)} %bitcast.2, bf16[32,2048]{1,0:T(8,128)(2,1)} %bitcast.3, bf16[1,8,2048]{2,1,0:T(8,128)(2,1)} %tk_in.1, ...), custom_call_target="tpu_custom_call" | custom-call | flops 1140850688 | bytes 8388608 | tf_op jit(solution)/shard_map/pallas_call | solution.py:425
  47.6 1.9 %copy.10 = bf16[1,1,2,64,2048]{4,3,2,1,0:T(8,128)(2,1)} copy(bf16[1,1,2,64,2048]{4,3,2,1,0:T(8,128)(2,1)} %shard_map.82) | data formatting | bytes 1048576

commit v5 on v4

--- a/solution.py
+++ b/solution.py
@@ -10,10 +10,10 @@
 
 HEADS = 16
 NEG_FILL = -1e30
-HEADS_PER_CHUNK = 1
+HEADS_PER_CHUNK = 2
 AHEAD = 3
-LOADS = 6
-FAR_LAG = 2
+LOADS = 5
+FAR_LAG = 1
 ATTEND_LAG = 3
 OWN, NEAR, FAR = 0, 1, 2
 
@@ -327,39 +327,39 @@
         def _():
             load_chunk(t + LOADS, 0)
 
+        @pl.when(t >= ATTEND_LAG)
+        def _():
+            g = t - ATTEND_LAG
+
+            @pl.when(g == 0)
+            def _():
+                for s in range(1, cols):
+                    top_copy(s).wait_recv()
+
+            @pl.when(has_left)
+            def _():
+                to_right(OWN, g).wait_recv()
+                to_right(NEAR, g).wait_recv()
+
+            @pl.when(has_right)
+            def _():
+                to_left(OWN, g).wait_recv()
+                to_left(NEAR, g).wait_recv()
+
+            @pl.when(has_far & has_left)
+            def _():
+                to_right(FAR, g).wait_recv()
+
+            @pl.when(has_far & has_right)
+            def _():
+                to_left(FAR, g).wait_recv()
+
+            attend(g)
+
         @pl.when((t >= FAR_LAG) & (t < chunks + FAR_LAG) & has_far)
         def _():
             far_copy(t - FAR_LAG).wait_recv()
             sideways(FAR, t - FAR_LAG)
-
-        @pl.when(t >= ATTEND_LAG)
-        def _():
-            g = t - ATTEND_LAG
-
-            @pl.when(g == 0)
-            def _():
-                for s in range(1, cols):
-                    top_copy(s).wait_recv()
-
-            @pl.when(has_left)
-            def _():
-                to_right(OWN, g).wait_recv()
-                to_right(NEAR, g).wait_recv()
-
-            @pl.when(has_right)
-            def _():
-                to_left(OWN, g).wait_recv()
-                to_left(NEAR, g).wait_recv()
-
-            @pl.when(has_far & has_left)
-            def _():
-                to_right(FAR, g).wait_recv()
-
-            @pl.when(has_far & has_right)
-            def _():
-                to_left(FAR, g).wait_recv()
-
-            attend(g)
 
         return 0
 

time: 49.7 us -> 45.3 us (0.911)
  Pallas kernels: 47.6 us -> 43.3 us
    pallas_call x1, Pallas kernels: 47.6 us -> 43.3 us  [body(): pl.pallas_call(functools.partial(kernel, dims), out_shape=jax.ShapeDtypeS...]
where the time goes in v5:
time: 45.3 us; the launch traced here: 45.2 us
  Pallas kernels  43.3 us (96%)
  local copies, waits for them, and re-layouts  1.88 us (4%)
    pallas_call x1, Pallas kernels, body(): pl.pallas_call(functools.partial(kernel, dims), out_shape=jax.ShapeDtypeS...  43.3 us
    unnamed x1, local copies, waits for them, and re-layouts  1.88 us

profile of v5, /device:TPU:5, one launch (start us, length us, event | category | flops | bytes accessed | tf_op | source)
XLA Modules:
  0.0 45.2 jit_solution(16105093969844472305)
XLA Ops:
  0.0 43.3 %shard_map.82 = bf16[1,1,2,64,2048]{4,3,2,1,0:T(8,128)(2,1)} custom-call(bf16[1,1,2,64,2048]{4,3,2,1,0:T(8,128)(2,1)} %q_in.1, bf16[1,1,2,64,2048]{4,3,2,1,0:T(8,128)(2,1)} %k_in.1, bf16[1,1,2,64,2048]{4,3,2,1,0:T(8,128)(2,1)} %v_in.1, bf16[32,2048]{1,0:T(8,128)(2,1)} %bitcast.2, bf16[32,2048]{1,0:T(8,128)(2,1)} %bitcast.3, bf16[1,8,2048]{2,1,0:T(8,128)(2,1)} %tk_in.1, ...), custom_call_target="tpu_custom_call" | custom-call | flops 1140850688 | bytes 8388608 | tf_op jit(solution)/shard_map/pallas_call | solution.py:425
  43.3 1.9 %copy.10 = bf16[1,1,2,64,2048]{4,3,2,1,0:T(8,128)(2,1)} copy(bf16[1,1,2,64,2048]{4,3,2,1,0:T(8,128)(2,1)} %shard_map.82) | data formatting | bytes 1048576

commit v6 on v5

v6 whole, which is shorter than its diff:
```python
import functools
import math

import jax
import jax.numpy as jnp
from jax import lax
from jax.experimental import pallas as pl
from jax.experimental.pallas import tpu as pltpu
from jax.sharding import PartitionSpec as P

HEADS = 16
NEG_FILL = -1e30
AHEAD = 2
LOADS = 3
FAR_LAG = 1
ATTEND_LAG = 2
MINE, MATE, BY_MINE, BY_MATE = range(4)


def kernel(
    dims,
    q_in,
    k_in,
    v_in,
    pk_in,
    pv_in,
    tk_in,
    tv_in,
    ids_in,
    out,
    own,
    give,
    left,
    right,
    back,
    top,
    top_own,
    ids,
    bias,
    load_sem,
    give_load_sem,
    top_sem,
    ids_sem,
    give_send,
    mate_recv,
    by_mine_send,
    by_mine_recv,
    by_mate_send,
    by_mate_recv,
    left_send,
    left_recv,
    right_send,
    right_recv,
    top_send,
    top_recv,
    bias_send,
    bias_recv,
    back_send,
    back_recv,
):
    rows, cols, tokens, pool_rows, pool_blocks, heads, width, listed_count = dims
    pool_tokens = pool_rows // pool_blocks
    r = lax.axis_index("row")
    c = lax.axis_index("col")
    odd = lax.rem(r, 2)
    mate = r + 1 - 2 * odd
    mine_to = r - 2 + 4 * odd
    mate_to = r + 2 - 4 * odd
    by_mine_row = r - 1 + 2 * odd
    has_by_mine = (mine_to >= 0) & (mine_to < rows)
    has_by_mate = (mate_to >= 0) & (mate_to < rows)
    has_left = c > 0
    has_right = c < cols - 1
    low = 2 * tokens
    mid = low + 2 * pool_rows
    full = mid + 2 * tokens
    edge = mid
    whole = full + 2 * tokens

    def lanes(half, h):
        return pl.ds(pl.multiple_of((half * heads + h) * width, width), width)

    def load_tile(half, h, tile, sem):
        at = lanes(half, h)
        pieces = (
            (k_in.at[pl.ds(0, tokens), at], 0, tokens),
            (v_in.at[pl.ds(0, tokens), at], tokens, tokens),
            (pk_in.at[:, at], low, pool_rows),
            (pv_in.at[:, at], low + pool_rows, pool_rows),
            (k_in.at[pl.ds(tokens, tokens), at], mid, tokens),
            (v_in.at[pl.ds(tokens, tokens), at], mid + tokens, tokens),
            (q_in.at[:, at], full, 2 * tokens),
        )
        for source, start, size in pieces:
            pltpu.make_async_copy(source, tile.at[pl.ds(start, size)], sem).start()

    def load(h):
        load_tile(1 - odd, h, give.at[h], give_load_sem.at[h])
        load_tile(odd, h, own.at[MINE, h], load_sem.at[h])

    barrier = pltpu.get_barrier_semaphore()

    def signal(row, col):
        pl.semaphore_signal(
            barrier, inc=1, device_id=(row, col), device_id_type=pl.DeviceIdType.MESH
        )

    signal(mate, c)

    @pl.when(r + 2 < rows)
    def _():
        signal(r + 2, c)

    @pl.when(r >= 2)
    def _():
        signal(r - 2, c)

    for step in range(1, cols):
        signal(r, lax.rem(c + step, cols))

    load(0)
    ids_copy = pltpu.make_async_copy(ids_in, ids, ids_sem)
    ids_copy.start()
    half_lanes = pl.ds(pl.multiple_of(odd * heads * width, heads * width), heads * width)
    tk_copy = pltpu.make_async_copy(tk_in.at[0, :, half_lanes], top_own.at[0], top_sem.at[0])
    tk_copy.start()
    tv_copy = pltpu.make_async_copy(tv_in.at[0, :, half_lanes], top_own.at[1], top_sem.at[1])
    tv_copy.start()
    for h in range(1, min(LOADS, heads)):
        load(h)

    greeted = 1 + (r + 2 < rows).astype(jnp.int32) + (r >= 2).astype(jnp.int32) + (cols - 1)
    pl.semaphore_wait(barrier, greeted)

    def remote(source, target, send, recv, row, col):
        return pltpu.make_async_remote_copy(
            src_ref=source,
            dst_ref=target,
            send_sem=send,
            recv_sem=recv,
            device_id=(row, col),
            device_id_type=pl.DeviceIdType.MESH,
        )

    def give_copy(h):
        return remote(give.at[h], own.at[MATE, h], give_send, mate_recv.at[h], mate, c)

    def by_mine_copy(h):
        return remote(
            own.at[MATE, h, pl.ds(0, full)],
            own.at[BY_MINE, h, pl.ds(0, full)],
            by_mine_send,
            by_mine_recv.at[h],
            mate_to,
            c,
        )

    def by_mate_copy(h):
        return remote(
            own.at[MINE, h, pl.ds(0, full)],
            own.at[BY_MATE, h, pl.ds(0, full)],
            by_mate_send,
            by_mate_recv.at[h],
            mine_to,
            c,
        )

    def to_left(k, h):
        return remote(
            own.at[k, h, pl.ds(0, edge)],
            right.at[k, h],
            left_send.at[k],
            right_recv.at[k, h],
            r,
            c - 1,
        )

    def to_right(k, h):
        return remote(
            own.at[k, h, pl.ds(full - edge, edge)],
            left.at[k, h],
            right_send.at[k],
            left_recv.at[k, h],
            r,
            c + 1,
        )

    def sideways(k, h):
        @pl.when(has_left)
        def _():
            to_left(k, h).start()

        @pl.when(has_right)
        def _():
            to_right(k, h).start()

    def top_copy(step):
        to = lax.rem(c + step, cols)
        return remote(top.at[c], top.at[c], top_send.at[step], top_recv.at[step], r, to)

    def back_copy(h):
        return remote(
            back.at[h], out.at[0, 0, :, :, lanes(odd, h)], back_send, back_recv, mate, c
        )

    bias_copy = remote(bias.at[MINE], bias.at[MATE], bias_send, bias_recv, mate, c)

    def send_own(h):
        pltpu.make_async_copy(give.at[h], give.at[h], give_load_sem.at[h]).wait()
        give_copy(h).start()
        pltpu.make_async_copy(own.at[MINE, h], own.at[MINE, h], load_sem.at[h]).wait()

        @pl.when(has_by_mine)
        def _():
            by_mate_copy(h).start()

        sideways(MINE, h)

    for h in range(min(AHEAD, heads)):
        send_own(h)
    tk_copy.wait()
    tv_copy.wait()
    ids_copy.wait()
    top[c] = jnp.concatenate(
        [top_own[0].astype(jnp.float32), top_own[1].astype(jnp.float32)], axis=0
    ).astype(jnp.bfloat16)
    for step in range(1, cols):
        top_copy(step).start()

    per = tk_in.shape[1]
    top_rows = cols * per
    for b in range(2):
        parts = []
        for row, row_there in ((r, True), (mate, True), (by_mine_row, has_by_mine)):
            for slot in range(4):
                if slot in (b, b + 1, b + 2):
                    there = jnp.logical_and(row_there, True)
                    if slot == 0:
                        there = there & has_left
                    if slot == 3:
                        there = there & has_right
                    value = jnp.where(there, 0.0, NEG_FILL)
                else:
                    value = jnp.float32(NEG_FILL)
                parts.append(jnp.full((1, tokens), value, jnp.float32))
            for shift in (-1, 0, 1):
                there = jnp.logical_and(row_there, (c + shift >= 0) & (c + shift < cols))
                base = (row * cols + c + shift) * pool_blocks
                for block in range(pool_blocks):
                    here = jnp.int32(0)
                    for n in range(ids.shape[3]):
                        here = here | (ids[0, 0, b, n] == base + block).astype(jnp.int32)
                    here = here * there.astype(jnp.int32)
                    value = (1.0 - here.astype(jnp.float32)) * NEG_FILL
                    parts.append(jnp.full((1, pool_tokens), value, jnp.float32))
        parts.append(jnp.zeros((1, top_rows), jnp.float32))
        at = 0
        for part in parts:
            bias[MINE, b : b + 1, at : at + part.shape[1]] = part
            at += part.shape[1]
    bias_copy.start()

    def clear(there, k):
        @pl.when(jnp.logical_not(there))
        def _():
            own[k, :, pl.ds(0, full)] = jnp.zeros((heads, full, width), own.dtype)

        @pl.when(jnp.logical_not(there & has_left))
        def _():
            left[k] = jnp.zeros(left.shape[1:], left.dtype)

        @pl.when(jnp.logical_not(there & has_right))
        def _():
            right[k] = jnp.zeros(right.shape[1:], right.dtype)

    for k in (MINE, MATE):
        @pl.when(jnp.logical_not(has_left))
        def _():
            left[k] = jnp.zeros(left.shape[1:], left.dtype)

        @pl.when(jnp.logical_not(has_right))
        def _():
            right[k] = jnp.zeros(right.shape[1:], right.dtype)

    clear(has_by_mine, BY_MINE)
    clear(has_by_mate, BY_MATE)

    score_scale = math.log2(math.e) / math.sqrt(width)

    def attend(h):
        at = pl.ds(pl.multiple_of(h * width, width), width)
        tops = top[:, :, at].astype(jnp.float32)
        top_k = tops[:, :per].reshape(top_rows, width).astype(jnp.bfloat16)
        top_v = tops[:, per:].reshape(top_rows, width).astype(jnp.bfloat16)
        side = full - edge

        def listed(slots, value):
            fine = tokens if value else 0
            pool = pool_rows if value else 0
            parts = []
            for k in slots:
                parts += [
                    left[k, h, pl.ds(mid + fine - side, tokens)],
                    own[k, h, pl.ds(fine, tokens)],
                    own[k, h, pl.ds(mid + fine, tokens)],
                    right[k, h, pl.ds(fine, tokens)],
                    left[k, h, pl.ds(low + pool - side, pool_rows)],
                    own[k, h, pl.ds(low + pool, pool_rows)],
                    right[k, h, pl.ds(low + pool, pool_rows)],
                ]
            parts.append(top_v if value else top_k)
            return jnp.concatenate(parts, axis=0)

        for slots in ((MATE, MINE, BY_MATE), (MINE, MATE, BY_MINE)):
            which = slots[0]
            scores = lax.dot_general(
                own[which, h, pl.ds(full, 2 * tokens)],
                listed(slots, False),
                (((1,), (1,)), ((), ())),
                preferred_element_type=jnp.float32,
            )
            added = bias[which, 0:2, 0:listed_count]
            scores = (scores * score_scale).reshape(2, tokens, -1) + added[:, None, :]
            peak = jnp.max(scores, axis=-1, keepdims=True)
            exponent = jnp.exp2(scores - peak)
            total = jnp.sum(exponent, axis=-1, keepdims=True)
            weights = (exponent * (1.0 / total)).astype(jnp.bfloat16)
            result = jnp.dot(
                weights.reshape(2 * tokens, -1),
                listed(slots, True),
                preferred_element_type=jnp.float32,
            )
            result = result.reshape(2, tokens, width).astype(jnp.bfloat16)
            if which == MATE:
                back[h] = result
                back_copy(h).start()
            else:
                out[0, 0, :, :, lanes(odd, h)] = result

    def step(t, _):
        @pl.when(t < heads)
        def _():
            give_copy(t).wait_recv()

            @pl.when(has_by_mate)
            def _():
                by_mine_copy(t).start()

            sideways(MATE, t)

        @pl.when(t + AHEAD < heads)
        def _():
            send_own(t + AHEAD)

        @pl.when(t + LOADS < heads)
        def _():
            load(t + LOADS)

        @pl.when(t >= ATTEND_LAG)
        def _():
            h = t - ATTEND_LAG

            @pl.when(h == 0)
            def _():
                bias_copy.wait_recv()
                for s in range(1, cols):
                    top_copy(s).wait_recv()

            for k, there in (
                (MINE, None),
                (MATE, None),
                (BY_MATE, has_by_mate),
                (BY_MINE, has_by_mine),
            ):
                @pl.when(has_left if there is None else there & has_left)
                def _():
                    to_right(k, h).wait_recv()

                @pl.when(has_right if there is None else there & has_right)
                def _():
                    to_left(k, h).wait_recv()

            attend(h)

        @pl.when((t >= FAR_LAG) & (t < heads + FAR_LAG))
        def _():
            h = t - FAR_LAG

            @pl.when(has_by_mate)
            def _():
                by_mate_copy(h).wait_recv()
                sideways(BY_MATE, h)

            @pl.when(has_by_mine)
            def _():
                by_mine_copy(h).wait_recv()
                sideways(BY_MINE, h)

        return 0

    lax.fori_loop(0, heads + ATTEND_LAG, step, 0)

    remote(give, own.at[MATE], give_send, mate_recv.at[0], mate, c).wait_send()
    bias_copy.wait_send()

    @pl.when(has_by_mate)
    def _():
        tiles = own.at[MATE, :, pl.ds(0, full)]
        remote(tiles, tiles, by_mine_send, by_mine_recv.at[0], mate_to, c).wait_send()

    @pl.when(has_by_mine)
    def _():
        tiles = own.at[MINE, :, pl.ds(0, full)]
        remote(tiles, tiles, by_mate_send, by_mate_recv.at[0], mine_to, c).wait_send()

    for k, there in ((MINE, None), (MATE, None), (BY_MATE, has_by_mate), (BY_MINE, has_by_mine)):
        @pl.when(has_left if there is None else there & has_left)
        def _():
            remote(
                right.at[k], right.at[k], left_send.at[k], right_recv.at[k, 0], r, c - 1
            ).wait_send()

        @pl.when(has_right if there is None else there & has_right)
        def _():
            remote(
                left.at[k], left.at[k], right_send.at[k], left_recv.at[k, 0], r, c + 1
            ).wait_send()

    for s in range(1, cols):
        top_copy(s).wait_send()
    returned = remote(back, back, back_send, back_recv, mate, c)
    returned.wait_send()
    returned.wait_recv()


def solution(mesh):
    row_count, col_count = mesh.shape["row"], mesh.shape["col"]

    def body(queries, keys, values, pool_keys, pool_values, top_keys, top_values, coarse_ids):
        tokens, model_width = queries.shape[3:]
        pool_blocks, pool_tokens, _ = pool_keys.shape
        pool_rows = pool_blocks * pool_tokens
        width = model_width // HEADS
        heads = HEADS // 2
        full = 4 * tokens + 2 * pool_rows
        edge = 2 * tokens + 2 * pool_rows
        whole = full + 2 * tokens
        per = top_keys.shape[1]
        listed = 3 * (4 * tokens + 3 * pool_rows) + col_count * per
        lanes = -(-listed // 128) * 128
        dims = (row_count, col_count, tokens, pool_rows, pool_blocks, heads, width, listed)
        dma = pltpu.SemaphoreType.DMA
        return pl.pallas_call(
            functools.partial(kernel, dims),
            out_shape=pltpu.VMEM(queries.shape, queries.dtype),
            in_specs=[pl.BlockSpec(memory_space=pltpu.HBM)] * 8,
            out_specs=pl.BlockSpec(memory_space=pltpu.VMEM),
            scratch_shapes=[
                pltpu.VMEM((4, heads, whole, width), jnp.bfloat16),
                pltpu.VMEM((heads, whole, width), jnp.bfloat16),
                pltpu.VMEM((4, heads, edge, width), jnp.bfloat16),
                pltpu.VMEM((4, heads, edge, width), jnp.bfloat16),
                pltpu.VMEM((heads, 2, tokens, width), jnp.bfloat16),
                pltpu.VMEM((col_count, 2 * per, model_width // 2), jnp.bfloat16),
                pltpu.VMEM((2, per, model_width // 2), jnp.bfloat16),
                pltpu.SMEM(coarse_ids.shape, jnp.int32),
                pltpu.VMEM((2, 8, lanes), jnp.float32),
                dma((heads,)),
                dma((heads,)),
                dma((2,)),
                dma,
                dma,
                dma((heads,)),
                dma,
                dma((heads,)),
                dma,
                dma((heads,)),
                dma((4,)),
                dma((4, heads)),
                dma((4,)),
                dma((4, heads)),
                dma((col_count,)),
                dma((col_count,)),
                dma,
                dma,
                dma,
                dma,
            ],
            compiler_params=pltpu.CompilerParams(
                collective_id=0, has_side_effects=True, vmem_limit_bytes=62 * 2**20
            ),
            cost_estimate=pl.CostEstimate(
                flops=4 * 2 * tokens * listed * model_width,
                bytes_accessed=8 * 2**20,
                transcendentals=2 * tokens * listed * HEADS,
            ),
        )(
            queries.reshape(2 * tokens, model_width),
            keys.reshape(2 * tokens, model_width),
            values.reshape(2 * tokens, model_width),
            pool_keys.reshape(pool_rows, model_width),
            pool_values.reshape(pool_rows, model_width),
            top_keys,
            top_values,
            coarse_ids,
        )

    placed = (
        P(None, "row", "col", None, None),
        P(None, "row", "col", None, None),
        P(None, "row", "col", None, None),
        P(("row", "col"), None, None),
        P(("row", "col"), None, None),
        P(None, "col", None),
        P(None, "col", None),
        P(None, "row", "col", None),
    )
    return jax.shard_map(
        body,
        mesh=mesh,
        in_specs=placed,
        out_specs=P(None, "row", "col", None, None),
        check_vma=False,
    )
```

time: 45.3 us -> 51.7 us (1.14)
  the two profiles are of different devices: /device:TPU:5 before, /device:TPU:18 now
where the time goes in v6:
time: 51.7 us; the launch traced here: 51.5 us
  Pallas kernels  50.7 us (98%)
  local copies, waits for them, and re-layouts  0.8 us (2%)
    pallas_call x1, Pallas kernels, body(): pl.pallas_call(functools.partial(kernel, dims), out_shape=pltpu.VMEM(quer...  50.7 us

profile of v6, /device:TPU:18, one launch (start us, length us, event | category | flops | bytes accessed | tf_op | source)
XLA Modules:
  0.0 51.5 jit_solution(7058948667351084350)
XLA Ops:
  0.0 50.7 %shard_map.82 = bf16[1,1,2,64,2048]{4,3,2,1,0:T(8,128)(2,1)S(1)} custom-call(bf16[128,2048]{1,0:T(8,128)(2,1)} %bitcast.5, bf16[128,2048]{1,0:T(8,128)(2,1)} %bitcast.6, bf16[128,2048]{1,0:T(8,128)(2,1)} %bitcast.7, bf16[32,2048]{1,0:T(8,128)(2,1)} %bitcast.8, bf16[32,2048]{1,0:T(8,128)(2,1)} %bitcast.9, bf16[1,8,2048]{2,1,0:T(8,128)(2,1)} %tk_in.1, ...), custom_call_target="tpu_custom_call" | custom-call | flops 1140850688 | bytes 8388608 | tf_op jit(solution)/shard_map/pallas_call | solution.py:453
  50.7 0.8 %copy.10 = bf16[1,1,2,64,2048]{4,3,2,1,0:T(8,128)(2,1)} copy(bf16[1,1,2,64,2048]{4,3,2,1,0:T(8,128)(2,1)S(1)} %shard_map.82) | data formatting | bytes 1048576

commit v7 on v5

--- a/solution.py
+++ b/solution.py
@@ -12,10 +12,10 @@
 NEG_FILL = -1e30
 HEADS_PER_CHUNK = 2
 AHEAD = 3
-LOADS = 5
 FAR_LAG = 1
 ATTEND_LAG = 3
-OWN, NEAR, FAR = 0, 1, 2
+PAIR = 2
+NEAR, FAR = 0, 1
 
 
 def kernel(
@@ -29,11 +29,13 @@
     tv_in,
     ids_in,
     out,
+    mine,
+    mine_left,
+    mine_right,
     own,
     left,
     right,
     q_buf,
-    out_buf,
     top,
     top_own,
     ids,
@@ -42,7 +44,6 @@
     top_sem,
     ids_sem,
     q_sem,
-    out_sem,
     near_send,
     near_recv,
     far_send,
@@ -51,6 +52,8 @@
     left_recv,
     right_send,
     right_recv,
+    mine_send,
+    mine_recv,
     top_send,
     top_recv,
 ):
@@ -74,21 +77,16 @@
     def lanes(g):
         return pl.ds(pl.multiple_of(g * width, width), width)
 
-    def load_chunk(g, _):
-        at = lanes(g)
-        pieces = (
-            (k_in.at[0, 0, 0, :, at], 0, tokens),
-            (v_in.at[0, 0, 0, :, at], tokens, tokens),
-            (k_in.at[0, 0, 1, :, at], mid, tokens),
-            (v_in.at[0, 0, 1, :, at], mid + tokens, tokens),
-            (pk_in.at[:, at], low, pool_rows),
-            (pv_in.at[:, at], low + pool_rows, pool_rows),
-        )
-        for source, start, size in pieces:
-            pltpu.make_async_copy(
-                source, own.at[OWN, g, pl.ds(start, size)], load_sem.at[g]
-            ).start()
-        return 0
+    pieces = (
+        (k_in.at[0, 0, 0], 0, tokens),
+        (v_in.at[0, 0, 0], tokens, tokens),
+        (pk_in, low, pool_rows),
+        (pv_in, low + pool_rows, pool_rows),
+        (k_in.at[0, 0, 1], mid, tokens),
+        (v_in.at[0, 0, 1], mid + tokens, tokens),
+    )
+    for source, start, size in pieces:
+        pltpu.make_async_copy(source, mine.at[pl.ds(start, size)], load_sem).start()
 
     barrier = pltpu.get_barrier_semaphore()
 
@@ -112,7 +110,6 @@
             device_id_type=pl.DeviceIdType.MESH,
         )
 
-    lax.fori_loop(0, min(LOADS, chunks), load_chunk, 0)
     ids_copy = pltpu.make_async_copy(ids_in, ids, ids_sem)
     ids_copy.start()
     tk_copy = pltpu.make_async_copy(tk_in.at[0], top_own.at[0], top_sem.at[0])
@@ -142,52 +139,64 @@
 
     def near_copy(g):
         return remote(
-            own.at[OWN, g], own.at[NEAR, g], near_send, near_recv.at[g], near_row, c
+            mine.at[:, lanes(g)], own.at[NEAR, g], near_send, near_recv.at[g], near_row, c
         )
 
     def far_copy(g):
         return remote(own.at[NEAR, g], own.at[FAR, g], far_send, far_recv.at[g], far_to, c)
 
-    def to_left(k, g):
+    def to_left(k, g, n):
         return remote(
-            own.at[k, g, pl.ds(0, edge)],
-            right.at[k, g],
+            own.at[k, pl.ds(g, n), pl.ds(0, edge)],
+            right.at[k, pl.ds(g, n)],
             left_send.at[k],
             right_recv.at[k, g],
             r,
             c - 1,
         )
 
-    def to_right(k, g):
+    def to_right(k, g, n):
         return remote(
-            own.at[k, g, pl.ds(full - edge, edge)],
-            left.at[k, g],
+            own.at[k, pl.ds(g, n), pl.ds(full - edge, edge)],
+            left.at[k, pl.ds(g, n)],
             right_send.at[k],
             left_recv.at[k, g],
             r,
             c + 1,
         )
 
-    def sideways(k, g):
+    def sideways(k, g, n):
         @pl.when(has_left)
         def _():
-            to_left(k, g).start()
+            to_left(k, g, n).start()
 
         @pl.when(has_right)
         def _():
-            to_right(k, g).start()
+            to_right(k, g, n).start()
+
+    mine_to_left = remote(
+        mine.at[pl.ds(0, edge)], mine_right, mine_send.at[0], mine_recv.at[1], r, c - 1
+    )
+    mine_to_right = remote(
+        mine.at[pl.ds(full - edge, edge)], mine_left, mine_send.at[1], mine_recv.at[0], r, c + 1
+    )
 
     def top_copy(step):
         to = lax.rem(c + step, cols)
         return remote(top.at[c], top.at[c], top_send.at[step], top_recv.at[step], r, to)
 
-    def send_own(g):
-        pltpu.make_async_copy(own.at[OWN, g], own.at[OWN, g], load_sem.at[g]).wait()
+    pltpu.make_async_copy(mine, mine, load_sem).wait()
+    for g in range(min(AHEAD, chunks)):
         near_copy(g).start()
-        sideways(OWN, g)
-
-    for g in range(min(AHEAD, chunks)):
-        send_own(g)
+
+    @pl.when(has_left)
+    def _():
+        mine_to_left.start()
+
+    @pl.when(has_right)
+    def _():
+        mine_to_right.start()
+
     tk_copy.wait()
     tv_copy.wait()
     ids_copy.wait()
@@ -212,18 +221,18 @@
 
     @pl.when(jnp.logical_not(has_left))
     def _():
-        for k in (OWN, NEAR):
-            left[k] = jnp.zeros(left.shape[1:], left.dtype)
+        left[NEAR] = jnp.zeros(left.shape[1:], left.dtype)
+        mine_left[...] = jnp.zeros(mine_left.shape, mine_left.dtype)
 
     @pl.when(jnp.logical_not(has_right))
     def _():
-        for k in (OWN, NEAR):
-            right[k] = jnp.zeros(right.shape[1:], right.dtype)
+        right[NEAR] = jnp.zeros(right.shape[1:], right.dtype)
+        mine_right[...] = jnp.zeros(mine_right.shape, mine_right.dtype)
 
     top_rows = cols * tk_in.shape[1]
     for b in range(2):
         parts = []
-        for k, row in ((OWN, r), (NEAR, near_row), (FAR, far_row)):
+        for row in (r, near_row, far_row):
             row_there = (row >= 0) & (row < rows)
             for slot in range(4):
                 if slot in (b, b + 1, b + 2):
@@ -271,8 +280,19 @@
             fine = tokens if value else 0
             pool = pool_rows if value else 0
             side = full - edge
-            parts = []
-            for k in (OWN, NEAR, FAR):
+            mine_lane = pl.ds(
+                pl.multiple_of(g * width + head * head_width, head_width), head_width
+            )
+            parts = [
+                mine_left[pl.ds(mid + fine - side, tokens), mine_lane],
+                mine[pl.ds(fine, tokens), mine_lane],
+                mine[pl.ds(mid + fine, tokens), mine_lane],
+                mine_right[pl.ds(fine, tokens), mine_lane],
+                mine_left[pl.ds(low + pool - side, pool_rows), mine_lane],
+                mine[pl.ds(low + pool, pool_rows), mine_lane],
+                mine_right[pl.ds(low + pool, pool_rows), mine_lane],
+            ]
+            for k in (NEAR, FAR):
                 parts += [
                     left[k, g, pl.ds(mid + fine - side, tokens), lane],
                     own[k, g, pl.ds(fine, tokens), lane],
@@ -303,10 +323,12 @@
                 listed(head, True, top_v),
                 preferred_element_type=jnp.float32,
             )
-            out_buf[g, :, :, head * head_width : (head + 1) * head_width] = result.reshape(
-                2, tokens, head_width
-            ).astype(jnp.bfloat16)
-        pltpu.make_async_copy(out_buf.at[g], out.at[0, 0, :, :, at], out_sem).start()
+            out_lane = pl.ds(
+                pl.multiple_of(g * width + head * head_width, head_width), head_width
+            )
+            out[0, 0, :, :, out_lane] = result.reshape(2, tokens, head_width).astype(
+                jnp.bfloat16
+            )
 
     def step(t, _):
         @pl.when(t < chunks)
@@ -317,15 +339,13 @@
             def _():
                 far_copy(t).start()
 
-            sideways(NEAR, t)
+            @pl.when(lax.rem(t, PAIR) == PAIR - 1)
+            def _():
+                sideways(NEAR, t - (PAIR - 1), PAIR)
 
         @pl.when(t + AHEAD < chunks)
         def _():
-            send_own(t + AHEAD)
-
-        @pl.when(t + LOADS < chunks)
-        def _():
-            load_chunk(t + LOADS, 0)
+            near_copy(t + AHEAD).start()
 
         @pl.when(t >= ATTEND_LAG)
         def _():
@@ -336,36 +356,44 @@
                 for s in range(1, cols):
                     top_copy(s).wait_recv()
 
-            @pl.when(has_left)
-            def _():
-                to_right(OWN, g).wait_recv()
-                to_right(NEAR, g).wait_recv()
-
-            @pl.when(has_right)
-            def _():
-                to_left(OWN, g).wait_recv()
-                to_left(NEAR, g).wait_recv()
+            @pl.when((g == 0) & has_left)
+            def _():
+                mine_to_right.wait_recv()
+
+            @pl.when((g == 0) & has_right)
+            def _():
+                mine_to_left.wait_recv()
+
+            first = lax.rem(g, PAIR) == 0
+
+            @pl.when(first & has_left)
+            def _():
+                to_right(NEAR, g, PAIR).wait_recv()
+
+            @pl.when(first & has_right)
+            def _():
+                to_left(NEAR, g, PAIR).wait_recv()
 
             @pl.when(has_far & has_left)
             def _():
-                to_right(FAR, g).wait_recv()
+                to_right(FAR, g, 1).wait_recv()
 
             @pl.when(has_far & has_right)
             def _():
-                to_left(FAR, g).wait_recv()
+                to_left(FAR, g, 1).wait_recv()
 
             attend(g)
 
         @pl.when((t >= FAR_LAG) & (t < chunks + FAR_LAG) & has_far)
         def _():
             far_copy(t - FAR_LAG).wait_recv()
-            sideways(FAR, t - FAR_LAG)
+            sideways(FAR, t - FAR_LAG, 1)
 
         return 0
 
     lax.fori_loop(0, chunks + ATTEND_LAG, step, 0)
 
-    remote(own.at[OWN], own.at[NEAR], near_send, near_recv.at[0], near_row, c).wait_send()
+    remote(own.at[NEAR], own.at[NEAR], near_send, near_recv.at[0], near_row, c).wait_send()
 
     @pl.when(has_to)
     def _():
@@ -394,7 +422,14 @@
                 c + 1,
             ).wait_send()
 
-    sent(OWN)
+    @pl.when(has_left)
+    def _():
+        mine_to_left.wait_send()
+
+    @pl.when(has_right)
+    def _():
+        mine_to_right.wait_send()
+
     sent(NEAR)
 
     @pl.when(has_far)
@@ -403,7 +438,6 @@
 
     for s in range(1, cols):
         top_copy(s).wait_send()
-    pltpu.make_async_copy(out_buf, out_buf, out_sem).wait()
 
 
 def solution(mesh):
@@ -424,37 +458,40 @@
         dma = pltpu.SemaphoreType.DMA
         return pl.pallas_call(
             functools.partial(kernel, dims),
-            out_shape=jax.ShapeDtypeStruct(queries.shape, queries.dtype),
+            out_shape=pltpu.VMEM(queries.shape, queries.dtype),
             in_specs=[pl.BlockSpec(memory_space=pltpu.HBM)] * 8,
-            out_specs=pl.BlockSpec(memory_space=pl.ANY),
+            out_specs=pl.BlockSpec(memory_space=pltpu.VMEM),
             scratch_shapes=[
-                pltpu.VMEM((3, chunks, full, width), jnp.bfloat16),
-                pltpu.VMEM((3, chunks, edge, width), jnp.bfloat16),
-                pltpu.VMEM((3, chunks, edge, width), jnp.bfloat16),
+                pltpu.VMEM((full, model_width), jnp.bfloat16),
+                pltpu.VMEM((edge, model_width), jnp.bfloat16),
+                pltpu.VMEM((edge, model_width), jnp.bfloat16),
+                pltpu.VMEM((2, chunks, full, width), jnp.bfloat16),
+                pltpu.VMEM((2, chunks, edge, width), jnp.bfloat16),
+                pltpu.VMEM((2, chunks, edge, width), jnp.bfloat16),
                 pltpu.VMEM((2, tokens, model_width), jnp.bfloat16),
-                pltpu.VMEM((chunks, 2, tokens, width), jnp.bfloat16),
                 pltpu.VMEM((col_count, 2 * per, model_width), jnp.bfloat16),
                 pltpu.VMEM((2, per, model_width), jnp.bfloat16),
                 pltpu.SMEM(coarse_ids.shape, jnp.int32),
                 pltpu.VMEM((2, listed), jnp.float32),
-                dma((chunks,)),
+                dma,
                 dma((2,)),
-                dma,
                 dma,
                 dma,
                 dma,
                 dma((chunks,)),
                 dma,
                 dma((chunks,)),
-                dma((3,)),
-                dma((3, chunks)),
-                dma((3,)),
-                dma((3, chunks)),
+                dma((2,)),
+                dma((2, chunks)),
+                dma((2,)),
+                dma((2, chunks)),
+                dma((2,)),
+                dma((2,)),
                 dma((col_count,)),
                 dma((col_count,)),
             ],
             compiler_params=pltpu.CompilerParams(
-                collective_id=0, has_side_effects=True, vmem_limit_bytes=63 * 2**20
+                collective_id=0, has_side_effects=True, vmem_limit_bytes=62 * 2**20
             ),
             cost_estimate=pl.CostEstimate(
                 flops=4 * 2 * tokens * listed * model_width,

time: 45.3 us -> 43.5 us (0.960)
  local copies, waits for them, and re-layouts: 1.88 us -> 0.8 us
  Pallas kernels: 43.3 us -> 42.5 us
    unnamed x1, local copies, waits for them, and re-layouts: 1.88 us -> 0.8 us
    pallas_call x1, Pallas kernels: 43.3 us -> 42.5 us  [body(): pl.pallas_call(functools.partial(kernel, dims), out_shape=pltpu.VMEM(quer...]
where the time goes in v7:
time: 43.5 us; the launch traced here: 43.3 us
  Pallas kernels  42.5 us (98%)
  local copies, waits for them, and re-layouts  0.8 us (2%)
    pallas_call x1, Pallas kernels, body(): pl.pallas_call(functools.partial(kernel, dims), out_shape=pltpu.VMEM(quer...  42.5 us

profile of v7, /device:TPU:5, one launch (start us, length us, event | category | flops | bytes accessed | tf_op | source)
XLA Modules:
  0.0 43.3 jit_solution(15864627703195261765)
XLA Ops:
  0.0 42.5 %shard_map.82 = bf16[1,1,2,64,2048]{4,3,2,1,0:T(8,128)(2,1)S(1)} custom-call(bf16[1,1,2,64,2048]{4,3,2,1,0:T(8,128)(2,1)} %q_in.1, bf16[1,1,2,64,2048]{4,3,2,1,0:T(8,128)(2,1)} %k_in.1, bf16[1,1,2,64,2048]{4,3,2,1,0:T(8,128)(2,1)} %v_in.1, bf16[32,2048]{1,0:T(8,128)(2,1)} %bitcast.2, bf16[32,2048]{1,0:T(8,128)(2,1)} %bitcast.3, bf16[1,8,2048]{2,1,0:T(8,128)(2,1)} %tk_in.1, ...), custom_call_target="tpu_custom_call" | custom-call | flops 1140850688 | bytes 8388608 | tf_op jit(solution)/shard_map/pallas_call | solution.py:459
  42.5 0.8 %copy.10 = bf16[1,1,2,64,2048]{4,3,2,1,0:T(8,128)(2,1)} copy(bf16[1,1,2,64,2048]{4,3,2,1,0:T(8,128)(2,1)S(1)} %shard_map.82) | data formatting | bytes 1048576

commit v8 on v7

--- a/solution.py
+++ b/solution.py
@@ -40,6 +40,7 @@
     top_own,
     ids,
     bias,
+    side_bias,
     load_sem,
     top_sem,
     ids_sem,
@@ -231,37 +232,32 @@
 
     top_rows = cols * tk_in.shape[1]
     for b in range(2):
-        parts = []
-        for row in (r, near_row, far_row):
-            row_there = (row >= 0) & (row < rows)
-            for slot in range(4):
-                if slot in (b, b + 1, b + 2):
-                    there = row_there
-                    if slot == 0:
-                        there = there & has_left
-                    if slot == 3:
-                        there = there & has_right
-                    value = jnp.where(there, 0.0, NEG_FILL)
-                else:
-                    value = jnp.float32(NEG_FILL)
-                parts.append(jnp.full((1, tokens), value, jnp.float32))
+        beside = has_left if b == 0 else has_right
+        far_beside = has_far & beside
+
+        def fine(there, count):
+            return jnp.full((1, count * tokens), jnp.where(there, 0.0, NEG_FILL), jnp.float32)
+
+        shared = []
+        for row, row_there, blocks in ((r, True, 1), (near_row, True, 2), (far_row, has_far, 2)):
+            shared.append(fine(row_there, blocks))
             for shift in (-1, 0, 1):
-                there = row_there & (c + shift >= 0) & (c + shift < cols)
+                there = jnp.logical_and(row_there, (c + shift >= 0) & (c + shift < cols))
                 base = (row * cols + c + shift) * pool_blocks
                 for block in range(pool_blocks):
-                    listed_here = jnp.int32(0)
+                    here = jnp.int32(0)
                     for n in range(ids.shape[3]):
-                        listed_here = listed_here | (ids[0, 0, b, n] == base + block).astype(
-                            jnp.int32
-                        )
-                    listed_here = listed_here * there.astype(jnp.int32)
-                    value = (1.0 - listed_here.astype(jnp.float32)) * NEG_FILL
-                    parts.append(jnp.full((1, pool_tokens), value, jnp.float32))
-        parts.append(jnp.zeros((1, top_rows), jnp.float32))
-        at = 0
-        for part in parts:
-            bias[b : b + 1, at : at + part.shape[1]] = part
-            at += part.shape[1]
+                        here = here | (ids[0, 0, b, n] == base + block).astype(jnp.int32)
+                    here = here * there.astype(jnp.int32)
+                    value = (1.0 - here.astype(jnp.float32)) * NEG_FILL
+                    shared.append(jnp.full((1, pool_tokens), value, jnp.float32))
+        shared.append(jnp.zeros((1, top_rows), jnp.float32))
+        private = [fine(beside, 2), fine(far_beside, 1), jnp.zeros((1, tokens), jnp.float32)]
+        for target, parts in ((bias, shared), (side_bias, private)):
+            at = 0
+            for part in parts:
+                target[b : b + 1, at : at + part.shape[1]] = part
+                at += part.shape[1]
 
     q_copy.wait()
 
@@ -275,60 +271,99 @@
         top_k = tops[:, :per].reshape(top_rows, width).astype(jnp.bfloat16)
         top_v = tops[:, per:].reshape(top_rows, width).astype(jnp.bfloat16)
 
-        def listed(head, value, top_part):
+        side = full - edge
+
+        def pieces_of(head, value):
             lane = pl.ds(head * head_width, head_width)
+            mine_lane = pl.ds(
+                pl.multiple_of(g * width + head * head_width, head_width), head_width
+            )
             fine = tokens if value else 0
             pool = pool_rows if value else 0
-            side = full - edge
-            mine_lane = pl.ds(
-                pl.multiple_of(g * width + head * head_width, head_width), head_width
-            )
-            parts = [
-                mine_left[pl.ds(mid + fine - side, tokens), mine_lane],
-                mine[pl.ds(fine, tokens), mine_lane],
-                mine[pl.ds(mid + fine, tokens), mine_lane],
-                mine_right[pl.ds(fine, tokens), mine_lane],
-                mine_left[pl.ds(low + pool - side, pool_rows), mine_lane],
-                mine[pl.ds(low + pool, pool_rows), mine_lane],
-                mine_right[pl.ds(low + pool, pool_rows), mine_lane],
+            top_part = top_v if value else top_k
+            first = pl.ds(fine, tokens)
+            second = pl.ds(mid + fine, tokens)
+            left_block = pl.ds(mid + fine - side, tokens)
+            left_pool = pl.ds(low + pool - side, pool_rows)
+            pools = pl.ds(low + pool, pool_rows)
+            mine_first = mine[first, mine_lane]
+            shared = [
+                mine[second, mine_lane],
+                mine_left[left_pool, mine_lane],
+                mine[pools, mine_lane],
+                mine_right[pools, mine_lane],
             ]
             for k in (NEAR, FAR):
-                parts += [
-                    left[k, g, pl.ds(mid + fine - side, tokens), lane],
-                    own[k, g, pl.ds(fine, tokens), lane],
-                    own[k, g, pl.ds(mid + fine, tokens), lane],
-                    right[k, g, pl.ds(fine, tokens), lane],
-                    left[k, g, pl.ds(low + pool - side, pool_rows), lane],
-                    own[k, g, pl.ds(low + pool, pool_rows), lane],
-                    right[k, g, pl.ds(low + pool, pool_rows), lane],
+                shared += [
+                    own[k, g, first, lane],
+                    own[k, g, second, lane],
+                    left[k, g, left_pool, lane],
+                    own[k, g, pools, lane],
+                    right[k, g, pools, lane],
                 ]
-            parts.append(top_part[:, head * head_width : (head + 1) * head_width])
-            return jnp.concatenate(parts, axis=0)
-
-        for head in range(width // head_width):
+            shared.append(top_part[:, head * head_width : (head + 1) * head_width])
+            low_side = [
+                mine_left[left_block, mine_lane],
+                left[NEAR, g, left_block, lane],
+                left[FAR, g, left_block, lane],
+                mine_first,
+            ]
+            high_side = [
+                mine_right[first, mine_lane],
+                right[NEAR, g, first, lane],
+                right[FAR, g, first, lane],
+                mine_first,
+            ]
+            return [jnp.concatenate(part, axis=0) for part in (shared, low_side, high_side)]
+
+        def product(x, y):
+            return lax.dot_general(
+                x, y, (((1,), (1,)), ((), ())), preferred_element_type=jnp.float32
+            )
+
+        def scores_of(head):
             q_head = q_chunk[:, head * head_width : (head + 1) * head_width]
-            scores = lax.dot_general(
-                q_head,
-                listed(head, False, top_k),
-                (((1,), (1,)), ((), ())),
-                preferred_element_type=jnp.float32,
-            )
-            scores = (scores * score_scale).reshape(2, tokens, -1) + bias[...][:, None, :]
-            peak = jnp.max(scores, axis=-1, keepdims=True)
-            exponent = jnp.exp2(scores - peak)
-            total = jnp.sum(exponent, axis=-1, keepdims=True)
-            weights = (exponent * (1.0 / total)).astype(jnp.bfloat16)
+            shared, low_side, high_side = pieces_of(head, False)
+            both = product(q_head, shared).reshape(2, tokens, -1)
+            alone = jnp.stack(
+                [product(q_head[:tokens], low_side), product(q_head[tokens:], high_side)]
+            )
+            return (
+                both * score_scale + bias[...][:, None, :],
+                alone * score_scale + side_bias[...][:, None, :],
+            )
+
+        def weights_of(both, alone):
+            peak = jnp.maximum(
+                jnp.max(both, axis=-1, keepdims=True), jnp.max(alone, axis=-1, keepdims=True)
+            )
+            both = jnp.exp2(both - peak)
+            alone = jnp.exp2(alone - peak)
+            total = jnp.sum(both, axis=-1, keepdims=True) + jnp.sum(alone, axis=-1, keepdims=True)
+            share = 1.0 / total
+            return (both * share).astype(jnp.bfloat16), (alone * share).astype(jnp.bfloat16)
+
+        def attended(head, both, alone):
+            shared, low_side, high_side = pieces_of(head, True)
             result = jnp.dot(
-                weights.reshape(2 * tokens, -1),
-                listed(head, True, top_v),
-                preferred_element_type=jnp.float32,
+                both.reshape(2 * tokens, -1), shared, preferred_element_type=jnp.float32
+            ).reshape(2, tokens, head_width)
+            result = result + jnp.stack(
+                [
+                    jnp.dot(alone[0], low_side, preferred_element_type=jnp.float32),
+                    jnp.dot(alone[1], high_side, preferred_element_type=jnp.float32),
+                ]
             )
             out_lane = pl.ds(
                 pl.multiple_of(g * width + head * head_width, head_width), head_width
             )
-            out[0, 0, :, :, out_lane] = result.reshape(2, tokens, head_width).astype(
-                jnp.bfloat16
-            )
+            out[0, 0, :, :, out_lane] = result.astype(jnp.bfloat16)
+
+        count = width // head_width
+        scores = [scores_of(head) for head in range(count)]
+        weights = [weights_of(*pair) for pair in scores]
+        for head in range(count):
+            attended(head, *weights[head])
 
     def step(t, _):
         @pl.when(t < chunks)
@@ -453,7 +488,7 @@
         full = 4 * tokens + 2 * pool_rows
         edge = 2 * tokens + 2 * pool_rows
         per = top_keys.shape[1]
-        listed = 3 * (4 * tokens + 3 * pool_rows) + col_count * per
+        listed = 5 * tokens + 9 * pool_rows + col_count * per
         dims = (row_count, col_count, tokens, pool_rows, pool_blocks, chunks, width, head_width)
         dma = pltpu.SemaphoreType.DMA
         return pl.pallas_call(
@@ -473,6 +508,7 @@
                 pltpu.VMEM((2, per, model_width), jnp.bfloat16),
                 pltpu.SMEM(coarse_ids.shape, jnp.int32),
                 pltpu.VMEM((2, listed), jnp.float32),
+                pltpu.VMEM((2, 4 * tokens), jnp.float32),
                 dma,
                 dma((2,)),
                 dma,
@@ -494,9 +530,9 @@
                 collective_id=0, has_side_effects=True, vmem_limit_bytes=62 * 2**20
             ),
             cost_estimate=pl.CostEstimate(
-                flops=4 * 2 * tokens * listed * model_width,
+                flops=4 * 2 * tokens * (listed + 4 * tokens) * model_width,
                 bytes_accessed=8 * 2**20,
-                transcendentals=2 * tokens * listed * HEADS,
+                transcendentals=2 * tokens * (listed + 4 * tokens) * HEADS,
             ),
         )(
             queries,

time: 43.5 us -> 43.1 us (level)
  no operation moved by 1% of the time
where the time goes in v8:
time: 43.1 us; the launch traced here: 42.9 us
  Pallas kernels  42.1 us (98%)
  local copies, waits for them, and re-layouts  0.8 us (2%)
    pallas_call x1, Pallas kernels, body(): pl.pallas_call(functools.partial(kernel, dims), out_shape=pltpu.VMEM(quer...  42.1 us

profile of v8, /device:TPU:5, one launch (start us, length us, event | category | flops | bytes accessed | tf_op | source)
XLA Modules:
  0.0 42.9 jit_solution(504451978169743957)
XLA Ops:
  0.0 42.1 %shard_map.82 = bf16[1,1,2,64,2048]{4,3,2,1,0:T(8,128)(2,1)S(1)} custom-call(bf16[1,1,2,64,2048]{4,3,2,1,0:T(8,128)(2,1)} %q_in.1, bf16[1,1,2,64,2048]{4,3,2,1,0:T(8,128)(2,1)} %k_in.1, bf16[1,1,2,64,2048]{4,3,2,1,0:T(8,128)(2,1)} %v_in.1, bf16[32,2048]{1,0:T(8,128)(2,1)} %bitcast.2, bf16[32,2048]{1,0:T(8,128)(2,1)} %bitcast.3, bf16[1,8,2048]{2,1,0:T(8,128)(2,1)} %tk_in.1, ...), custom_call_target="tpu_custom_call" | custom-call | flops 939524096 | bytes 8388608 | tf_op jit(solution)/shard_map/pallas_call | solution.py:494
  42.1 0.8 %copy.10 = bf16[1,1,2,64,2048]{4,3,2,1,0:T(8,128)(2,1)} copy(bf16[1,1,2,64,2048]{4,3,2,1,0:T(8,128)(2,1)S(1)} %shard_map.82) | data formatting | bytes 1048576

commit v9 on v8

--- a/solution.py
+++ b/solution.py
@@ -175,12 +175,37 @@
         def _():
             to_right(k, g, n).start()
 
-    mine_to_left = remote(
-        mine.at[pl.ds(0, edge)], mine_right, mine_send.at[0], mine_recv.at[1], r, c - 1
-    )
-    mine_to_right = remote(
-        mine.at[pl.ds(full - edge, edge)], mine_left, mine_send.at[1], mine_recv.at[0], r, c + 1
-    )
+    def piece(p):
+        return pl.ds(pl.multiple_of(p * PAIR * width, PAIR * width), PAIR * width)
+
+    def mine_to_left(p):
+        return remote(
+            mine.at[pl.ds(0, edge), piece(p)],
+            mine_right.at[:, piece(p)],
+            mine_send.at[0],
+            mine_recv.at[1, p],
+            r,
+            c - 1,
+        )
+
+    def mine_to_right(p):
+        return remote(
+            mine.at[pl.ds(full - edge, edge), piece(p)],
+            mine_left.at[:, piece(p)],
+            mine_send.at[1],
+            mine_recv.at[0, p],
+            r,
+            c + 1,
+        )
+
+    def mine_sideways(p):
+        @pl.when(has_left)
+        def _():
+            mine_to_left(p).start()
+
+        @pl.when(has_right)
+        def _():
+            mine_to_right(p).start()
 
     def top_copy(step):
         to = lax.rem(c + step, cols)
@@ -190,14 +215,7 @@
     for g in range(min(AHEAD, chunks)):
         near_copy(g).start()
 
-    @pl.when(has_left)
-    def _():
-        mine_to_left.start()
-
-    @pl.when(has_right)
-    def _():
-        mine_to_right.start()
-
+    mine_sideways(0)
     tk_copy.wait()
     tv_copy.wait()
     ids_copy.wait()
@@ -378,6 +396,10 @@
             def _():
                 sideways(NEAR, t - (PAIR - 1), PAIR)
 
+            @pl.when((lax.rem(t, PAIR) == PAIR - 1) & (t + 1 < chunks))
+            def _():
+                mine_sideways((t + 1) // PAIR)
+
         @pl.when(t + AHEAD < chunks)
         def _():
             near_copy(t + AHEAD).start()
@@ -391,22 +413,16 @@
                 for s in range(1, cols):
                     top_copy(s).wait_recv()
 
-            @pl.when((g == 0) & has_left)
-            def _():
-                mine_to_right.wait_recv()
-
-            @pl.when((g == 0) & has_right)
-            def _():
-                mine_to_left.wait_recv()
-
             first = lax.rem(g, PAIR) == 0
 
             @pl.when(first & has_left)
             def _():
+                mine_to_right(g // PAIR).wait_recv()
                 to_right(NEAR, g, PAIR).wait_recv()
 
             @pl.when(first & has_right)
             def _():
+                mine_to_left(g // PAIR).wait_recv()
                 to_left(NEAR, g, PAIR).wait_recv()
 
             @pl.when(has_far & has_left)
@@ -459,11 +475,15 @@
 
     @pl.when(has_left)
     def _():
-        mine_to_left.wait_send()
+        remote(
+            mine_right, mine_right, mine_send.at[0], mine_recv.at[1, 0], r, c - 1
+        ).wait_send()
 
     @pl.when(has_right)
     def _():
-        mine_to_right.wait_send()
+        remote(
+            mine_left, mine_left, mine_send.at[1], mine_recv.at[0, 0], r, c + 1
+        ).wait_send()
 
     sent(NEAR)
 
@@ -522,7 +542,7 @@
                 dma((2,)),
                 dma((2, chunks)),
                 dma((2,)),
-                dma((2,)),
+                dma((2, chunks // PAIR)),
                 dma((col_count,)),
                 dma((col_count,)),
             ],

time: 43.1 us -> 43.1 us (level)
  no operation moved by 1% of the time
where the time goes in v9:
time: 43.1 us; the launch traced here: 43 us
  Pallas kernels  42.2 us (98%)
  local copies, waits for them, and re-layouts  0.8 us (2%)
    pallas_call x1, Pallas kernels, body(): pl.pallas_call(functools.partial(kernel, dims), out_shape=pltpu.VMEM(quer...  42.2 us

profile of v9, /device:TPU:5, one launch (start us, length us, event | category | flops | bytes accessed | tf_op | source)
XLA Modules:
  0.0 43.0 jit_solution(13566465046549898427)
XLA Ops:
  0.0 42.2 %shard_map.82 = bf16[1,1,2,64,2048]{4,3,2,1,0:T(8,128)(2,1)S(1)} custom-call(bf16[1,1,2,64,2048]{4,3,2,1,0:T(8,128)(2,1)} %q_in.1, bf16[1,1,2,64,2048]{4,3,2,1,0:T(8,128)(2,1)} %k_in.1, bf16[1,1,2,64,2048]{4,3,2,1,0:T(8,128)(2,1)} %v_in.1, bf16[32,2048]{1,0:T(8,128)(2,1)} %bitcast.2, bf16[32,2048]{1,0:T(8,128)(2,1)} %bitcast.3, bf16[1,8,2048]{2,1,0:T(8,128)(2,1)} %tk_in.1, ...), custom_call_target="tpu_custom_call" | custom-call | flops 939524096 | bytes 8388608 | tf_op jit(solution)/shard_map/pallas_call | solution.py:514
  42.2 0.8 %copy.10 = bf16[1,1,2,64,2048]{4,3,2,1,0:T(8,128)(2,1)} copy(bf16[1,1,2,64,2048]{4,3,2,1,0:T(8,128)(2,1)S(1)} %shard_map.82) | data formatting | bytes 1048576

commit v10 on v9

--- a/solution.py
+++ b/solution.py
@@ -10,9 +10,9 @@
 
 HEADS = 16
 NEG_FILL = -1e30
-HEADS_PER_CHUNK = 2
-AHEAD = 3
-FAR_LAG = 1
+HEADS_PER_CHUNK = 1
+AHEAD = 5
+FAR_LAG = 2
 ATTEND_LAG = 3
 PAIR = 2
 NEAR, FAR = 0, 1
@@ -167,13 +167,13 @@
         )
 
     def sideways(k, g, n):
+        @pl.when(has_right)
+        def _():
+            to_right(k, g, n).start()
+
         @pl.when(has_left)
         def _():
             to_left(k, g, n).start()
-
-        @pl.when(has_right)
-        def _():
-            to_right(k, g, n).start()
 
     def piece(p):
         return pl.ds(pl.multiple_of(p * PAIR * width, PAIR * width), PAIR * width)

time: 43.1 us -> 66.4 us (1.54); the launches traced: 43 us -> 65.5 us
  Pallas kernels: 42.2 us -> 64.7 us
    pallas_call x1, Pallas kernels: 42.2 us -> 64.7 us  [body(): pl.pallas_call(functools.partial(kernel, dims), out_shape=pltpu.VMEM(quer...]
where the time goes in v10:
time: 66.4 us; the launch traced here: 65.5 us
  Pallas kernels  64.7 us (97%)
  local copies, waits for them, and re-layouts  0.8 us (1%)
    pallas_call x1, Pallas kernels, body(): pl.pallas_call(functools.partial(kernel, dims), out_shape=pltpu.VMEM(quer...  64.7 us

profile of v10, /device:TPU:5, one launch (start us, length us, event | category | flops | bytes accessed | tf_op | source)
XLA Modules:
  0.0 65.5 jit_solution(3821553456067867378)
XLA Ops:
  0.0 64.7 %shard_map.82 = bf16[1,1,2,64,2048]{4,3,2,1,0:T(8,128)(2,1)S(1)} custom-call(bf16[1,1,2,64,2048]{4,3,2,1,0:T(8,128)(2,1)} %q_in.1, bf16[1,1,2,64,2048]{4,3,2,1,0:T(8,128)(2,1)} %k_in.1, bf16[1,1,2,64,2048]{4,3,2,1,0:T(8,128)(2,1)} %v_in.1, bf16[32,2048]{1,0:T(8,128)(2,1)} %bitcast.2, bf16[32,2048]{1,0:T(8,128)(2,1)} %bitcast.3, bf16[1,8,2048]{2,1,0:T(8,128)(2,1)} %tk_in.1, ...), custom_call_target="tpu_custom_call" | custom-call | flops 939524096 | bytes 8388608 | tf_op jit(solution)/shard_map/pallas_call | solution.py:514
  64.7 0.8 %copy.10 = bf16[1,1,2,64,2048]{4,3,2,1,0:T(8,128)(2,1)} copy(bf16[1,1,2,64,2048]{4,3,2,1,0:T(8,128)(2,1)S(1)} %shard_map.82) | data formatting | bytes 1048576

commit v11 on v8

--- a/solution.py
+++ b/solution.py
@@ -30,6 +30,7 @@
     ids_in,
     out,
     mine,
+    pack,
     mine_left,
     mine_right,
     own,
@@ -42,6 +43,7 @@
     bias,
     side_bias,
     load_sem,
+    pack_sem,
     top_sem,
     ids_sem,
     q_sem,
@@ -140,7 +142,7 @@
 
     def near_copy(g):
         return remote(
-            mine.at[:, lanes(g)], own.at[NEAR, g], near_send, near_recv.at[g], near_row, c
+            pack.at[g], own.at[NEAR, g], near_send, near_recv.at[g], near_row, c
         )
 
     def far_copy(g):
@@ -187,8 +189,18 @@
         return remote(top.at[c], top.at[c], top_send.at[step], top_recv.at[step], r, to)
 
     pltpu.make_async_copy(mine, mine, load_sem).wait()
+
+    def pack_copy(g):
+        return pltpu.make_async_copy(mine.at[:, lanes(g)], pack.at[g], pack_sem.at[g])
+
+    def send_near(g):
+        pack_copy(g).wait()
+        near_copy(g).start()
+
+    for g in range(chunks):
+        pack_copy(g).start()
     for g in range(min(AHEAD, chunks)):
-        near_copy(g).start()
+        send_near(g)
 
     @pl.when(has_left)
     def _():
@@ -380,7 +392,7 @@
 
         @pl.when(t + AHEAD < chunks)
         def _():
-            near_copy(t + AHEAD).start()
+            send_near(t + AHEAD)
 
         @pl.when(t >= ATTEND_LAG)
         def _():
@@ -498,6 +510,7 @@
             out_specs=pl.BlockSpec(memory_space=pltpu.VMEM),
             scratch_shapes=[
                 pltpu.VMEM((full, model_width), jnp.bfloat16),
+                pltpu.VMEM((chunks, full, width), jnp.bfloat16),
                 pltpu.VMEM((edge, model_width), jnp.bfloat16),
                 pltpu.VMEM((edge, model_width), jnp.bfloat16),
                 pltpu.VMEM((2, chunks, full, width), jnp.bfloat16),
@@ -510,6 +523,7 @@
                 pltpu.VMEM((2, listed), jnp.float32),
                 pltpu.VMEM((2, 4 * tokens), jnp.float32),
                 dma,
+                dma((chunks,)),
                 dma((2,)),
                 dma,
                 dma,

time: 43.1 us -> 43.3 us (level)
  no operation moved by 1% of the time
where the time goes in v11:
time: 43.3 us; the launch traced here: 43.2 us
  Pallas kernels  42.4 us (98%)
  local copies, waits for them, and re-layouts  0.8 us (2%)
    pallas_call x1, Pallas kernels, body(): pl.pallas_call(functools.partial(kernel, dims), out_shape=pltpu.VMEM(quer...  42.4 us

profile of v11, /device:TPU:5, one launch (start us, length us, event | category | flops | bytes accessed | tf_op | source)
XLA Modules:
  0.0 43.2 jit_solution(14919507555504934001)
XLA Ops:
  0.0 42.4 %shard_map.82 = bf16[1,1,2,64,2048]{4,3,2,1,0:T(8,128)(2,1)S(1)} custom-call(bf16[1,1,2,64,2048]{4,3,2,1,0:T(8,128)(2,1)} %q_in.1, bf16[1,1,2,64,2048]{4,3,2,1,0:T(8,128)(2,1)} %k_in.1, bf16[1,1,2,64,2048]{4,3,2,1,0:T(8,128)(2,1)} %v_in.1, bf16[32,2048]{1,0:T(8,128)(2,1)} %bitcast.2, bf16[32,2048]{1,0:T(8,128)(2,1)} %bitcast.3, bf16[1,8,2048]{2,1,0:T(8,128)(2,1)} %tk_in.1, ...), custom_call_target="tpu_custom_call" | custom-call | flops 939524096 | bytes 8388608 | tf_op jit(solution)/shard_map/pallas_call | solution.py:506
  42.4 0.8 %copy.10 = bf16[1,1,2,64,2048]{4,3,2,1,0:T(8,128)(2,1)} copy(bf16[1,1,2,64,2048]{4,3,2,1,0:T(8,128)(2,1)S(1)} %shard_map.82) | data formatting | bytes 1048576
